TPU v7x, 128 devices: a whole 4x4x4 slice. The times are simulated.
128 devices in a mesh: group: 8 (over x_lo, y), inner: 16 (over x_hi, z, core).
Axes of the slice: x: 4 (x_hi: 2, x_lo: 2; x = x_hi * 2 + x_lo), y: 4, z: 4, core: 2. Of those that a mesh axis runs over, the one named last changes fastest.
Arguments:
- visits: bfloat16 [65536, 1024], P(('group', 'inner')), may hold values from -6 to 6
- enc_weight: bfloat16 [1024, 1024], replicated, may hold values from -0.1875 to 0.1875
- drug_table: bfloat16 [4096, 1024], P(('group', 'inner')), may hold values from -0.59765625 to 0.59765625
- labels: int32 [65536, 32], P(('group', 'inner')), may hold values from 0 to 4095, as said below
- drug_order: int32 [4096], replicated, may hold values from 0 to 4095, each once
Outputs:
- drug_grad: float32 [4096, 1024], P(('group', 'inner'))
- weight_grad: float32 [1024, 1024], replicated
Inputs may be any that keep to these rules, and one draw needn't show every extreme that they name: `labels`: each visit lists 32 different catalogue ids; the id in column j lies in [j * 128, (j + 1) * 128); every id of the window is listed by some visit. `drug_order`: A permutation of the catalogue ids.
All inputs are finite; a program needn't handle non-finite values.
Results may differ from a plain program's by a relative error of at most 0.00093.
Values may be sent and summed in bfloat16 or wider, within the bound.
A program may use at most 128 MiB of HBM per device.

v0:
```python
import math

import jax
import jax.numpy as jnp
from jax import lax
from jax.sharding import PartitionSpec as P


def local_term(columns, coded):
    term = lax.dot_general(
        columns, coded, (((0,), (0,)), ((), ())), preferred_element_type=jnp.float32
    )
    return lax.optimization_barrier(term.astype(jnp.bfloat16)).astype(jnp.float32)


def local(visits, enc_weight, drug_table, labels, drug_order):
    n_group = lax.axis_size("group")
    n_inner = lax.axis_size("inner")
    visit_rows = visits.shape[0]
    loss_scale = 1.0 / math.sqrt(visit_rows * n_group * n_inner)
    hidden = jnp.dot(visits, enc_weight, preferred_element_type=jnp.float32)
    squash = jnp.tanh(hidden)
    coded = squash.astype(jnp.bfloat16)
    piece = lax.all_gather(drug_table, ("group", "inner"), axis=0, tiled=True)
    logits = lax.dot_general(
        coded, piece, (((1,), (1,)), ((), ())), preferred_element_type=jnp.float32
    )
    matches = labels[:, :, None] == drug_order[None, None, :]
    labelled = jnp.any(matches, axis=1).astype(jnp.float32)
    update = (loss_scale * (jax.nn.sigmoid(logits) - labelled)).astype(jnp.bfloat16)
    coded_grad = jnp.dot(update, piece, preferred_element_type=jnp.float32)
    residual, coded_grad = (update, coded_grad)
    shares = lax.psum_scatter(local_term(residual, coded), "group", scatter_dimension=0, tiled=True)
    drug_grad = lax.psum_scatter(shares, "inner", scatter_dimension=0, tiled=True)
    hidden_grad = (coded_grad * (1.0 - squash * squash)).astype(jnp.bfloat16)
    weight_part = lax.dot_general(
        visits, hidden_grad, (((0,), (0,)), ((), ())), preferred_element_type=jnp.float32
    )
    weight_grad = lax.psum(weight_part, ("group", "inner"))
    return (drug_grad, weight_grad)


def solution(mesh):
    return jax.shard_map(
        local,
        mesh=mesh,
        in_specs=(
            P(("group", "inner"), None),
            P(),
            P(("group", "inner"), None),
            P(("group", "inner"), None),
            P(),
        ),
        out_specs=(P(("group", "inner"), None), P()),
        check_vma=False,
    )
```

profile of v0, /device:TPU:1, one launch (start us, length us, event | category | flops | bytes accessed | tf_op | source)
XLA Modules:
  0.0 653.1 jit_solution(3240278304821672171)
XLA Ops:
  7.2 0.0 copy-start
  7.2 0.0 copy-start.1
  7.2 0.0 all-gather.2.cloned.1.call-start
  7.2 0.7 all-gather.2.cloned.1.call-update
  7.9 0.0 reduce-scatter.3.cloned.1.call-start
  8.0 1.0 copy.9
  8.9 0.0 copy-done
  8.9 3.8 fusion.1
  12.8 0.0 copy-done.1
  12.8 58.8 %compare_reduce_fusion = pred[512,4096]{1,0:T(8,128)(4,1)} fusion(s32[4096]{0:T(1024)S(1)} %copy-done.1, s32[512,32]{1,0:T(8,128)S(1)} %copy.9), kind=kLoop, calls=%fused_computation | loop fusion | flops 132120576 | bytes 2179072 | tf_op jit(solution)/shard_map/reduce_or | solution.py:29
  71.6 144.3 %all-gather.2.cloned.1.call-done = bf16[4096,1024]{1,0:T(8,128)(2,1)} async-done(((bf16[32,1024]{1,0:T(8,128)(2,1)}), bf16[4096,1024]{1,0:T(8,128)(2,1)}) %all-gather.2.cloned.1.call-update) | async-done | bytes 8388624 | tf_op jit(solution)/shard_map/all_gather | solution.py:24
  215.9 0.0 copy-start.3
  215.9 10.6 %multiply_convert_fusion = bf16[512,4096]{1,0:T(8,128)(2,1)S(1)} fusion(pred[512,4096]{1,0:T(8,128)(4,1)} %compare_reduce_fusion, bf16[4096,1024]{1,0:T(8,128)(2,1)} %all-gather.2.cloned.1.call-done, f32[512,1024]{1,0:T(8,128)} %fusion.1), kind=kOutput, calls=%fused_computation.1 | convolution fusion | flops 4310171648 | bytes 16777216 | tf_op jit(solution)/shard_map/dot_general | solution.py:25
  226.5 0.0 copy-start.4
  226.5 2.0 copy-done.4
  228.5 0.0 copy-done.3
  228.5 6.8 %convolution_convert_fusion = bf16[4096,1024]{1,0:T(8,128)(2,1)} fusion(bf16[512,4096]{1,0:T(8,128)(2,1)S(1)} %multiply_convert_fusion, f32[512,1024]{1,0:T(8,128)S(1)} %copy-done.3), kind=kOutput, calls=%fused_computation.2 | convolution fusion | flops 4299685888 | bytes 14680064 | tf_op jit(solution)/shard_map/dot_general | solution.py:10
  235.4 11.3 %convert_element_type.22 = f32[4096,1024]{1,0:T(8,128)} convert(bf16[4096,1024]{1,0:T(8,128)(2,1)} %convolution_convert_fusion) | non-fusion elementwise | flops 4194304 | bytes 25165824 | tf_op jit(solution)/shard_map/convert_element_type | solution.py:13
  246.6 0.0 copy-start.2
  246.6 0.0 reduce-scatter.3.cloned.1.call-update
  246.7 0.2 all-reduce.2.cloned.1.call-start
  246.9 1.0 copy-done.2
  247.9 12.7 %convolution_bitcast_fusion = f32[1024,1024]{0,1:T(8,128)} fusion(bf16[512,1024]{1,0:T(8,128)(2,1)S(1)} %copy-done.2, f32[512,1024]{1,0:T(8,128)} %fusion.1, bf16[512,4096]{1,0:T(8,128)(2,1)} %copy-done.4, bf16[4096,1024]{1,0:T(8,128)(2,1)} %all-gather.2.cloned.1.call-done), kind=kOutput, calls=%fused_computation.3 | convolution fusion | flops 5370806272 | bytes 19922944 | tf_op jit(solution)/shard_map/dot_general | solution.py:36
  260.6 0.0 all-reduce.2.cloned.1.call-update
  260.6 0.0 reduce-scatter.5.cloned.1.call-start
  260.7 156.2 %reduce-scatter.3.cloned.1.call-done = f32[512,1024]{1,0:T(8,128)} async-done(((f32[4096,1024]{1,0:T(8,128)}), f32[512,1024]{1,0:T(8,128)}) %reduce-scatter.3.cloned.1.call-update) | async-done | bytes 2097168 | tf_op jit(solution)/shard_map/reduce_scatter | solution.py:33
  416.9 0.0 reduce-scatter.5.cloned.1.call-update
  416.9 157.8 %all-reduce.2.cloned.1.call-done = f32[1024,1024]{0,1:T(8,128)} async-done(((f32[1024,1024]{0,1:T(8,128)}), f32[1024,1024]{0,1:T(8,128)}) %all-reduce.2.cloned.1.call-update) | async-done | bytes 4194320 | tf_op jit(solution)/shard_map/psum | solution.py:39
  574.8 5.3 copy.10
  580.1 66.5 %reduce-scatter.5.cloned.1.call-done = f32[32,1024]{1,0:T(8,128)} async-done(((f32[512,1024]{1,0:T(8,128)}), f32[32,1024]{1,0:T(8,128)}) %reduce-scatter.5.cloned.1.call-update) | async-done | bytes 131088 | tf_op jit(solution)/shard_map/reduce_scatter | solution.py:34
Async XLA Ops:
  7.2 1.8 copy-start
  7.2 5.6 copy-start.1
  7.2 208.7 %all-gather.2.cloned.1.call-start = ((), (), s32[]{:S(2)}) async-start(), calls=%async_computation.2 | async-start | bytes 8454144 | tf_op jit(solution)/shard_map/all_gather | solution.py:24
  7.9 409.0 %reduce-scatter.3.cloned.1.call-start = ((), (), s32[]{:S(2)}) async-start(), calls=%async_computation.3 | async-start | bytes 18874368 | tf_op jit(solution)/shard_map/reduce_scatter | solution.py:33
  215.9 12.7 %copy-start.3 = (f32[512,1024]{1,0:T(8,128)S(1)}, f32[512,1024]{1,0:T(8,128)}, u32[]{:S(2)}) copy-start(f32[512,1024]{1,0:T(8,128)} %fusion.1) | copy-start | bytes 6291460
  226.5 2.0 copy-start.4
  246.6 1.2 copy-start.2
  246.7 328.1 %all-reduce.2.cloned.1.call-start = ((), (), s32[]{:S(2)}) async-start(), calls=%async_computation.5 | async-start | bytes 8388608 | tf_op jit(solution)/shard_map/psum | solution.py:39
  260.6 386.0 %reduce-scatter.5.cloned.1.call-start = ((), (), s32[]{:S(2)}) async-start(), calls=%async_computation.4 | async-start | bytes 2228224 | tf_op jit(solution)/shard_map/reduce_scatter | solution.py:34
Sparse Core Ops, SparseCore 0:
  9.7 206.0 all-gather.1
  246.8 170.0 reduce-scatter.2
  421.8 152.8 all-reduce.1
  579.1 67.5 reduce-scatter.4
where the time goes:
time: 655 us; the launch traced here: 653 us
  waiting for transfers between devices  526 us (80%)
  other arithmetic  70.1 us (11%)
  matrix products  34 us (5%)
  between operations  13.8 us (2%)
  local copies, waits for them, and re-layouts  9.29 us (1%)
    psum x1, waiting for transfers between devices, local(): weight_grad = lax.psum(weight_part, ('group', 'inner'))  158 us
    reduce_scatter x1, waiting for transfers between devices, local(): lax.psum_scatter(local_term(residual, coded), 'group', scatter_dimension=...  156 us
    all_gather x1, waiting for transfers between devices, local(): piece = lax.all_gather(drug_table, ('group', 'inner'), axis=0, tiled=True)  144 us
    reduce_scatter x1, waiting for transfers between devices, local(): lax.psum_scatter(shares, 'inner', scatter_dimension=0, tiled=True)  66.5 us
    reduce_or x1, other arithmetic, local(): labelled = jnp.any(matches, axis=1).astype(jnp.float32)  58.8 us
  transfers between devices with their start and end apart: 4, of which 4 were waited for; matrix products, arithmetic and copies ran while one was open for 13% of the time, Pallas kernels for 0%

commit v1 on v0

v1 whole, which is shorter than its diff:
```python
import math

import jax
import jax.numpy as jnp
from jax import lax
from jax.experimental import pallas as pl
from jax.experimental.pallas import tpu as pltpu
from jax.sharding import PartitionSpec as P

MESH = pl.DeviceIdType.MESH
F32 = jnp.float32
BF16 = jnp.bfloat16
NN = (((1,), (0,)), ((), ()))
NT = (((1,), (1,)), ((), ()))

PARTS = ((0, 1, 2), (1, 2, 0), (2, 0, 1))
COLS = ((0, 384), (384, 384), (768, 256))
OFFS = (1, -1, 2)
REL = (0, 1, -1, 2)


def mod4(v):
    return lax.rem(v + 8, 4)


def kernel(
    visits, weight, table, labels, order, dgrad, wgrad,
    vis, vis_t, w_half, w_t, own_order, own_labels, order_t, sel, lab, coded, squash, tab, tab_t, res,
    cg_out, cg_in, cg_own, hgrad,
    s0, s1, s2, fp0, fp1, fp2, own0, own1, own2, hb0, hb1, hb2, rb0, rb1, rb2, r2b0, r2b1, r2b2, r2s0, r2s1, r2s2,
    r3b0, r3b1, r3b2,
    wfull, wlow, w1b0, w1b1, w1b2, wp0, wp1, wp2, w2b0, w2b1, w2b2, wq0, wq1, wq2, w3b0, w3b1, w3b2, wout,
    load_sem, ag_s, ag_r, rs_s, rs_r, wt_s, wt_r, d2d_s, d2d_r, out_l, out_s, out_r,
):
    g, i = lax.axis_index("group"), lax.axis_index("inner")
    x = (i // 8) * 2 + g // 4
    y = lax.rem(g, 4)
    z = lax.rem(i // 2, 4)
    core = lax.rem(i, 2)
    pos = (x, y, z)

    def device(px, py, pz, pc):
        return (lax.rem(px, 2) * 4 + py, (px // 2) * 8 + pz * 2 + pc)

    def peer(axis, off):
        moved = [mod4(v + off) if k == axis else v for k, v in enumerate(pos)]
        return device(*moved, core)

    sibling = device(x, y, z, 1 - core)
    sends = []

    def send(src, dst, ssem, rsem, to):
        copy = pltpu.make_async_remote_copy(
            src_ref=src, dst_ref=dst, send_sem=ssem, recv_sem=rsem, device_id=to, device_id_type=MESH
        )
        copy.start()
        sends.append(copy)

    def received(dst, ssem, rsem, to):
        pltpu.make_async_remote_copy(
            src_ref=dst, dst_ref=dst, send_sem=ssem, recv_sem=rsem, device_id=to, device_id_type=MESH
        ).wait_recv()

    def cols(p):
        return pl.ds(COLS[p][0], COLS[p][1])

    def row_of(buf, p, b_at, c_at):
        a, b, c = PARTS[p]
        at = [None, None, None]
        at[a], at[b], at[c] = slice(None), b_at, c_at
        return buf.at[at[2], at[1], at[0], :, cols(p)]

    def block_of(buf, p, a_at, b_at, c_at):
        a, b, c = PARTS[p]
        at = [None, None, None]
        at[a], at[b], at[c] = a_at, b_at, c_at
        return buf.at[at[2], at[1], at[0], :, cols(p)]

    def plane_row(buf, p, b_at):
        return buf.at[:, b_at] if p == 2 else buf.at[b_at]

    mine = pl.ds(pl.multiple_of(core * 512, 512), 512)
    theirs = pl.ds(pl.multiple_of((1 - core) * 512, 512), 512)
    loads = [
        pltpu.make_async_copy(table, tab.at[z, y, x], load_sem.at[0]),
        pltpu.make_async_copy(weight.at[:, mine], w_half, load_sem.at[1]),
        pltpu.make_async_copy(visits, vis.at[mine], load_sem.at[2]),
        pltpu.make_async_copy(labels, own_labels, load_sem.at[3]),
        pltpu.make_async_copy(order, own_order, load_sem.at[4]),
    ]
    for load in loads:
        load.start()
    barrier = pltpu.get_barrier_semaphore()
    partners = [peer(axis, off) for axis in range(3) for off in OFFS] + [sibling]
    for partner in partners:
        pl.semaphore_signal(barrier, inc=1, device_id=partner, device_id_type=MESH)
    pl.semaphore_wait(barrier, len(partners))

    for k, off in enumerate(OFFS):
        for p in range(3):
            a, b, c = PARTS[p]
            send(table.at[:, cols(p)], block_of(tab, p, pos[a], pos[b], pos[c]), ag_s.at[p, k], ag_r.at[p, k], peer(a, off))
    send(visits, vis.at[mine], d2d_s.at[0], d2d_r.at[0], sibling)

    loads[3].wait()
    lane = lax.broadcasted_iota(jnp.int32, (512, 32), 1)
    lab[mine, :] = jnp.concatenate(
        [
            (own_labels[...] - lane * 128).astype(F32),
            jnp.ones((512, 1), F32),
            jnp.zeros((512, 95), F32),
        ],
        axis=1,
    ).astype(BF16)
    send(lab.at[mine], lab.at[mine], d2d_s.at[1], d2d_r.at[1], sibling)
    loads[1].wait()
    w_t[...] = w_half[...].T
    loads[0].wait()
    for p in range(3):
        a, b, c = PARTS[p]
        for k, off in enumerate(OFFS):
            received(block_of(tab, p, mod4(pos[a] - off), pos[b], pos[c]), ag_s.at[p, k], ag_r.at[p, k], peer(a, off))

    def send_row_c(p, j, b_at):
        a, b, c = PARTS[p]
        row = row_of(tab, p, b_at, pos[c])
        for d, off in enumerate((1, -1)):
            send(row, row, ag_s.at[p, 6 + 2 * j + d], ag_r.at[p, 6 + 2 * j + d], peer(c, off))

    for p in range(3):
        a, b, c = PARTS[p]
        row = row_of(tab, p, pos[b], pos[c])
        for k, off in enumerate(OFFS):
            send(row, row, ag_s.at[p, 3 + k], ag_r.at[p, 3 + k], peer(b, off))
        send_row_c(p, 0, pos[b])

    def hidden_of(rows):
        hidden = lax.dot_general(w_t[...], vis[rows, :], NT, preferred_element_type=F32)
        value = jnp.tanh(hidden)
        squash[:, rows] = value
        coded[mine, rows] = value.astype(BF16)

    loads[2].wait()
    hidden_of(mine)

    for k, off in enumerate(OFFS):
        for p in range(3):
            a, b, c = PARTS[p]
            b_at = mod4(pos[b] - off)
            received(row_of(tab, p, b_at, pos[c]), ag_s.at[p, 3 + k], ag_r.at[p, 3 + k], peer(b, off))
            send_row_c(p, REL.index(-off if off != 2 else 2), b_at)

    received(vis.at[theirs], d2d_s.at[0], d2d_r.at[0], sibling)
    hidden_of(theirs)
    send(coded.at[mine], coded.at[mine], d2d_s.at[2], d2d_r.at[2], sibling)

    def take_row(j):
        for p in range(3):
            a, b, c = PARTS[p]
            b_at = mod4(pos[b] + REL[j])
            low = row_of(tab, p, b_at, mod4(pos[c] - 1))
            received(low, ag_s.at[p, 6 + 2 * j], ag_r.at[p, 6 + 2 * j], peer(c, 1))
            if j in (0, 1):
                send(low, low, ag_s.at[p, 14 + j], ag_r.at[p, 14 + j], peer(c, 1))
            high = row_of(tab, p, b_at, mod4(pos[c] + 1))
            received(high, ag_s.at[p, 7 + 2 * j], ag_r.at[p, 7 + 2 * j], peer(c, -1))
            if j in (2, 3):
                send(high, high, ag_s.at[p, 14 + j], ag_r.at[p, 14 + j], peer(c, -1))

    take_row(0)
    loads[4].wait()
    order_t[...] = own_order[...].astype(F32).T
    lane_q = lax.broadcasted_iota(jnp.int32, (32, 32), 1)
    lane_j = lax.broadcasted_iota(jnp.int32, (32, 128), 1)

    def select(n, _):
        bz, by, bx = n // 16, lax.rem(n // 4, 4), lax.rem(n, 4)
        q = (lax.rem(bx, 2) * 4 + by) * 4 + (bx // 2) * 2 + bz // 2
        m = lax.rem(bz, 2) * 2 + core
        rows = order_t[pl.ds(pl.multiple_of(m * 32, 32), 32), :]
        ids = jnp.sum(jnp.where(lane_q == q, rows, 0.0), axis=1, keepdims=True).astype(jnp.int32)
        ids = jnp.broadcast_to(ids, (32, 128))
        picked = jnp.where(lane_j == (ids >> 7), 1.0, 0.0)
        sel[n] = jnp.where(lane_j == 32, -(ids & 127).astype(F32), picked).astype(BF16)
        return 0

    lax.fori_loop(0, 64, select, 0)
    take_row(2)
    vis_t[...] = vis[...].T
    take_row(1)
    take_row(3)
    received(coded.at[theirs], d2d_s.at[2], d2d_r.at[2], sibling)
    received(lab.at[theirs], d2d_s.at[1], d2d_r.at[1], sibling)
    for j in (0, 1, 2, 3):
        for p in range(3):
            a, b, c = PARTS[p]
            row = row_of(tab, p, mod4(pos[b] + REL[j]), mod4(pos[c] + 2))
            received(row, ag_s.at[p, 14 + j], ag_r.at[p, 14 + j], peer(c, 1 if j < 2 else -1))

    scale = 1.0 / 256.0

    def residual_of(n, _):
        plane, half = n // 2, lax.rem(n, 2)
        seen = pl.ds(pl.multiple_of(half * 512, 512), 512)
        rows = tab[plane].reshape(512, 1024)
        logits = lax.dot_general(rows, coded[:, seen], NN, preferred_element_type=F32)
        gap = lax.dot_general(
            sel[pl.ds(plane * 16, 16)].reshape(512, 128), lab[seen, :], NT, preferred_element_type=F32
        )
        prob = 0.5 * jnp.tanh(0.5 * logits) + 0.5
        value = (prob - jnp.where(gap == 0.0, 1.0, 0.0)) * scale
        res[plane, :, :, :, seen] = value.astype(BF16).reshape(4, 4, 32, 512)
        return 0

    lax.fori_loop(0, 8, residual_of, 0)

    s, fp, own = (s0, s1, s2), (fp0, fp1, fp2), (own0, own1, own2)
    hb, rb = (hb0, hb1, hb2), (rb0, rb1, rb2)
    r2b, r2s, r3b = (r2b0, r2b1, r2b2), (r2s0, r2s1, r2s2), (r3b0, r3b1, r3b2)

    def term(p, off):
        c_at = mod4(pos[PARTS[p][2]] + off)
        rows = (res[c_at], res[:, :, c_at], res[:, c_at])[p].reshape(512, 1024)
        value = lax.dot_general(rows, coded[cols(p), :], NT, preferred_element_type=F32)
        return value.reshape(4, 4, 32, COLS[p][1])

    for p in range(3):
        a, b, c = PARTS[p]
        s[p][2] = term(p, 2).astype(BF16)
        for j in range(4):
            src = plane_row(s[p].at[2], p, mod4(pos[b] + REL[j]))
            send(src, hb[p].at[j], rs_s.at[p, j], rs_r.at[p, j], peer(c, 1 if j < 2 else -1))

    def send_term_row(p, k, j):
        b, c = PARTS[p][1], PARTS[p][2]
        src = plane_row(s[p].at[k], p, mod4(pos[b] + REL[j]))
        send(src, rb[p].at[k, j], rs_s.at[p, 4 + 4 * k + j], rs_r.at[p, 4 + 4 * k + j], peer(c, OFFS[k]))

    for k in range(2):
        for p in range(3):
            a, b, c = PARTS[p]
            value = term(p, OFFS[k])
            fp[p][k] = value
            s[p][k] = value.astype(BF16)
            for j in (2, 3) if k == 0 else (0, 1):
                send_term_row(p, k, j)
    for p in range(3):
        own[p][...] = term(p, 0)

    for j in (0, 2, 1, 3):
        k = 0 if j < 2 else 1
        for p in range(3):
            a, b, c = PARTS[p]
            received(hb[p].at[j], rs_s.at[p, j], rs_r.at[p, j], peer(c, 1 if j < 2 else -1))
            b_at = mod4(pos[b] + REL[j])
            whole = plane_row(fp[p].at[k], p, b_at)[...] + hb[p][j].astype(F32)
            plane_row(s[p].at[k], p, b_at)[...] = whole.astype(BF16)
            send_term_row(p, k, j)

    def transposed(n, _):
        tab_t[:, pl.ds(pl.multiple_of(n * 512, 512), 512)] = tab[n].reshape(512, 1024).T
        return 0

    lax.fori_loop(0, 4, transposed, 0)
    flat = res.reshape(2048, 1024)

    def coded_grad(at):
        rows = tab_t[pl.ds(pl.multiple_of(at, 128), 128), :]
        return lax.dot_general(rows, flat[...], NN, preferred_element_type=F32)

    def away(n, _):
        cg_out[pl.ds(pl.multiple_of(n * 128, 128), 128), :] = coded_grad((1 - core) * 512 + n * 128).astype(BF16)
        return 0

    lax.fori_loop(0, 4, away, 0)
    send(cg_out, cg_in, d2d_s.at[3], d2d_r.at[3], sibling)

    def home(n, _):
        cg_own[pl.ds(pl.multiple_of(n * 128, 128), 128), :] = coded_grad(core * 512 + n * 128)
        return 0

    lax.fori_loop(0, 4, home, 0)
    received(cg_in, d2d_s.at[3], d2d_r.at[3], sibling)
    hgrad[...] = ((cg_own[...] + cg_in[...].astype(F32)) * (1.0 - squash[...] * squash[...])).astype(BF16)

    for half in range(2):
        value = lax.dot_general(vis_t[pl.ds(half * 512, 512), :], hgrad[...], NT, preferred_element_type=F32)
        wfull[:, pl.ds(half * 512, 512)] = value
        wlow[:, pl.ds(half * 512, 512)] = value.astype(BF16)
    w1b, wp, w2b, wq, w3b = (
        (w1b0, w1b1, w1b2), (wp0, wp1, wp2), (w2b0, w2b1, w2b2), (wq0, wq1, wq2), (w3b0, w3b1, w3b2)
    )

    def span(at, size):
        return pl.ds(pl.multiple_of(at * size, size), size)

    for k, off in enumerate(OFFS):
        for p in range(3):
            c = PARTS[p][2]
            src = wlow.at[span(mod4(pos[c] + off), 128), cols(p)]
            send(src, w1b[p].at[k], wt_s.at[p, k], wt_r.at[p, k], peer(c, off))

    for p in range(3):
        a, b, c = PARTS[p]
        for j in (2, 0, 1, 3):
            for k in range(2):
                received(rb[p].at[k, j], rs_s.at[p, 4 + 4 * k + j], rs_r.at[p, 4 + 4 * k + j], peer(c, OFFS[k]))
            mine_row = plane_row(own[p], p, mod4(pos[b] + REL[j]))
            mine_row[...] = mine_row[...] + rb[p][0, j].astype(F32) + rb[p][1, j].astype(F32)
        for k, off in enumerate(OFFS):
            src = plane_row(own[p], p, mod4(pos[b] + off))
            send(src, r2b[p].at[k], rs_s.at[p, 12 + k], rs_r.at[p, 12 + k], peer(b, off))

    for p in range(3):
        c = PARTS[p][2]
        for k, off in enumerate(OFFS):
            received(w1b[p].at[k], wt_s.at[p, k], wt_r.at[p, k], peer(c, off))
        wp[p][...] = (
            wfull[span(pos[c], 128), cols(p)]
            + w1b[p][0].astype(F32) + w1b[p][1].astype(F32) + w1b[p][2].astype(F32)
        )
        b = PARTS[p][1]
        for k, off in enumerate(OFFS):
            src = wp[p].at[span(mod4(pos[b] + off), 32)]
            send(src, w2b[p].at[k], wt_s.at[p, 3 + k], wt_r.at[p, 3 + k], peer(b, off))

    for p in range(3):
        a, b, c = PARTS[p]
        for k, off in enumerate(OFFS):
            received(r2b[p].at[k], rs_s.at[p, 12 + k], rs_r.at[p, 12 + k], peer(b, off))
        r2s[p][...] = plane_row(own[p], p, pos[b])[...] + r2b[p][0] + r2b[p][1] + r2b[p][2]
        for k, off in enumerate(OFFS):
            send(r2s[p].at[mod4(pos[a] + off)], r3b[p].at[k], rs_s.at[p, 15 + k], rs_r.at[p, 15 + k], peer(a, off))

    for p in range(3):
        a, b, c = PARTS[p]
        for k, off in enumerate(OFFS):
            received(w2b[p].at[k], wt_s.at[p, 3 + k], wt_r.at[p, 3 + k], peer(b, off))
        wq[p][...] = wp[p][span(pos[b], 32), :] + w2b[p][0] + w2b[p][1] + w2b[p][2]
        for k, off in enumerate(OFFS):
            src = wq[p].at[span(mod4(pos[a] + off), 8)]
            send(src, w3b[p].at[k], wt_s.at[p, 6 + k], wt_r.at[p, 6 + k], peer(a, off))

    for p in range(3):
        a, b, c = PARTS[p]
        for k, off in enumerate(OFFS):
            received(w3b[p].at[k], wt_s.at[p, 6 + k], wt_r.at[p, 6 + k], peer(a, off))
        at = span((pos[c] * 4 + pos[b]) * 4 + pos[a], 8)
        wout[at, cols(p)] = wq[p][span(pos[a], 8), :] + w3b[p][0] + w3b[p][1] + w3b[p][2]
        for k, off in enumerate(OFFS):
            block = wout.at[at, cols(p)]
            send(block, block, wt_s.at[p, 9 + k], wt_r.at[p, 9 + k], peer(a, off))

    for p in range(3):
        a, b, c = PARTS[p]
        for k, off in enumerate(OFFS):
            received(r3b[p].at[k], rs_s.at[p, 15 + k], rs_r.at[p, 15 + k], peer(a, off))
        dgrad[:, cols(p)] = r2s[p][pos[a]] + r3b[p][0] + r3b[p][1] + r3b[p][2]

    for p in range(3):
        a, b, c = PARTS[p]
        for k, off in enumerate(OFFS):
            block = wout.at[span((pos[c] * 4 + pos[b]) * 4 + mod4(pos[a] - off), 8), cols(p)]
            received(block, wt_s.at[p, 9 + k], wt_r.at[p, 9 + k], peer(a, off))
        for k, off in enumerate(OFFS):
            row = wout.at[span(pos[c] * 4 + pos[b], 32), cols(p)]
            send(row, row, wt_s.at[p, 12 + k], wt_r.at[p, 12 + k], peer(b, off))

    pieces = (((0, 0, 0, 384),), ((1, 384, 0, 128), (2, 512, 1, 256)), ((3, 768, 1, 256),))
    locals_ = []

    def deliver(p, n, c_at):
        for q, lo, half, size in pieces[p]:
            src = wout.at[span(c_at, 128), pl.ds(lo, size)]
            dst = wgrad.at[
                pl.ds(pl.multiple_of(half * 512 + c_at * 128, 128), 128),
                pl.ds(pl.multiple_of(core * 512 + lo - half * 512, 128), size),
            ]
            copy = pltpu.make_async_copy(src, dst, out_l.at[q, n])
            copy.start()
            locals_.append(copy)
            send(src, dst, out_s.at[q, n], out_r.at[q, n], sibling)

    for p in range(3):
        a, b, c = PARTS[p]
        for k, off in enumerate(OFFS):
            row = wout.at[span(pos[c] * 4 + mod4(pos[b] - off), 32), cols(p)]
            received(row, wt_s.at[p, 12 + k], wt_r.at[p, 12 + k], peer(b, off))
        plane = wout.at[span(pos[c], 128), cols(p)]
        for k, off in enumerate((1, -1)):
            send(plane, plane, wt_s.at[p, 15 + k], wt_r.at[p, 15 + k], peer(c, off))
        deliver(p, 0, pos[c])
    for p in range(3):
        c = PARTS[p][2]
        for k, off in enumerate((1, -1)):
            at = mod4(pos[c] - off)
            received(wout.at[span(at, 128), cols(p)], wt_s.at[p, 15 + k], wt_r.at[p, 15 + k], peer(c, off))
            half = wout.at[span(at * 2 + k, 64), cols(p)]
            send(half, half, wt_s.at[p, 17 + k], wt_r.at[p, 17 + k], peer(c, off))
            deliver(p, 1 + k, at)
    for p in range(3):
        c = PARTS[p][2]
        at = mod4(pos[c] + 2)
        for k, off in enumerate((1, -1)):
            received(wout.at[span(at * 2 + k, 64), cols(p)], wt_s.at[p, 17 + k], wt_r.at[p, 17 + k], peer(c, off))
        deliver(p, 3, at)
    for p in range(3):
        c = PARTS[p][2]
        for n, off in enumerate((0, -1, 1, 2)):
            c_at = mod4(pos[c] + off)
            for q, lo, half, size in pieces[p]:
                dst = wgrad.at[
                    pl.ds(pl.multiple_of(half * 512 + c_at * 128, 128), 128),
                    pl.ds(pl.multiple_of((1 - core) * 512 + lo - half * 512, 128), size),
                ]
                received(dst, out_s.at[q, n], out_r.at[q, n], sibling)
    for copy in sends:
        copy.wait_send()
    for copy in locals_:
        copy.wait()


def per_part(make):
    return [make(width) for _, width in COLS]


def local(visits, enc_weight, drug_table, labels, drug_order):
    vmem = pltpu.VMEM
    scratch = [
        vmem((1024, 1024), BF16), vmem((1024, 1024), BF16), vmem((1024, 512), BF16), vmem((512, 1024), BF16),
        vmem((32, 128), jnp.int32), vmem((512, 32), jnp.int32), vmem((128, 32), F32),
        vmem((64, 32, 128), BF16), vmem((1024, 128), BF16), vmem((1024, 1024), BF16), vmem((512, 1024), F32),
        vmem((4, 4, 4, 32, 1024), BF16), vmem((1024, 2048), BF16), vmem((4, 4, 4, 32, 1024), BF16),
        vmem((512, 1024), BF16), vmem((512, 1024), BF16), vmem((512, 1024), F32), vmem((512, 1024), BF16),
        *per_part(lambda n: vmem((3, 4, 4, 32, n), BF16)),
        *per_part(lambda n: vmem((2, 4, 4, 32, n), F32)),
        *per_part(lambda n: vmem((4, 4, 32, n), F32)),
        *per_part(lambda n: vmem((4, 4, 32, n), BF16)),
        *per_part(lambda n: vmem((2, 4, 4, 32, n), BF16)),
        *per_part(lambda n: vmem((3, 4, 32, n), F32)),
        *per_part(lambda n: vmem((4, 32, n), F32)),
        *per_part(lambda n: vmem((3, 32, n), F32)),
        vmem((512, 1024), F32), vmem((512, 1024), BF16),
        *per_part(lambda n: vmem((3, 128, n), BF16)),
        *per_part(lambda n: vmem((128, n), F32)),
        *per_part(lambda n: vmem((3, 32, n), F32)),
        *per_part(lambda n: vmem((32, n), F32)),
        *per_part(lambda n: vmem((3, 8, n), F32)),
        vmem((512, 1024), F32),
        pltpu.SemaphoreType.DMA((5,)),
        pltpu.SemaphoreType.DMA((3, 18)), pltpu.SemaphoreType.DMA((3, 18)),
        pltpu.SemaphoreType.DMA((3, 18)), pltpu.SemaphoreType.DMA((3, 18)),
        pltpu.SemaphoreType.DMA((3, 19)), pltpu.SemaphoreType.DMA((3, 19)),
        pltpu.SemaphoreType.DMA((4,)), pltpu.SemaphoreType.DMA((4,)),
        pltpu.SemaphoreType.DMA((4, 4)), pltpu.SemaphoreType.DMA((4, 4)), pltpu.SemaphoreType.DMA((4, 4)),
    ]
    anywhere = pl.BlockSpec(memory_space=pl.ANY)
    return pl.pallas_call(
        kernel,
        name="step",
        out_shape=(jax.ShapeDtypeStruct((32, 1024), F32), jax.ShapeDtypeStruct((1024, 1024), F32)),
        in_specs=[anywhere] * 5,
        out_specs=(pl.BlockSpec(memory_space=pltpu.VMEM), anywhere),
        scratch_shapes=scratch,
        compiler_params=pltpu.CompilerParams(
            collective_id=0, has_side_effects=True, vmem_limit_bytes=60 * 2**20
        ),
    )(visits, enc_weight, drug_table, labels, drug_order.reshape(32, 128))


def solution(mesh):
    return jax.shard_map(
        local,
        mesh=mesh,
        in_specs=(
            P(("group", "inner"), None),
            P(),
            P(("group", "inner"), None),
            P(("group", "inner"), None),
            P(),
        ),
        out_specs=(P(("group", "inner"), None), P()),
        check_vma=False,
    )
```

time: 655 us -> 112 us (0.17)
  waiting for transfers between devices: 526 us -> 0 us
  Pallas kernels: 0 us -> 103 us
  other arithmetic: 70.1 us -> 0 us
  matrix products: 34 us -> 0 us
  between operations: 13.8 us -> 0.64 us
    reduce_scatter x2 -> x0, waiting for transfers between devices: 223 us -> none  [the longest x1 156 us: local(): lax.psum_scatter(local_term(residual, coded), 'group', scatter_dimension=...]
    psum x1 -> x0, waiting for transfers between devices: 158 us -> none  [local(): weight_grad = lax.psum(weight_part, ('group', 'inner'))]
    all_gather x1 -> x0, waiting for transfers between devices: 144 us -> none  [local(): piece = lax.all_gather(drug_table, ('group', 'inner'), axis=0, tiled=True)]
    pallas_call x0 -> x1, Pallas kernels: none -> 103 us  [local(): pl.pallas_call(kernel, name='step', out_shape=(jax.ShapeDtypeStruct((32,...]
    reduce_or x1 -> x0, other arithmetic: 58.8 us -> none  [local(): labelled = jnp.any(matches, axis=1).astype(jnp.float32)]
    dot_general x4 -> x0, matrix products: 34 us -> none  [the longest x1 12.7 us: local(): lax.dot_general(visits, hidden_grad, (((0,), (0,)), ((), ())), preferred_...]
    convert_element_type x1 -> x0, other arithmetic: 11.3 us -> none  [local_term(): lax.optimization_barrier(term.astype(jnp.bfloat16)).astype(jnp.float32)]
  transfers between devices with their start and end apart: 4 -> 0, of which waited for: 4 -> 0; matrix products, arithmetic and copies ran while one was open for 13% -> 0% of each run, Pallas kernels for 0% -> 0%
where the time goes in v1:
time: 112 us
  Pallas kernels  103 us (92%)
  local copies, waits for them, and re-layouts  8.03 us (7%)
    pallas_call x1, Pallas kernels, local(): pl.pallas_call(kernel, name='step', out_shape=(jax.ShapeDtypeStruct((32,...  103 us
    unnamed x3, local copies, waits for them, and re-layouts  8.03 us

profile of v1, /device:TPU:1, one launch (start us, length us, event | category | flops | bytes accessed | tf_op | source)
XLA Modules:
  0.0 111.6 jit_solution(15633369444316791397)
XLA Ops:
  0.6 1.7 %copy.7.labels = s32[512,32]{1,0:T(8,128)} copy(s32[512,32]{0,1:T(8,128)} %param.8) | data formatting | bytes 131072 | tf_op args[3]
  2.3 102.9 %step.1 = (f32[32,1024]{1,0:T(8,128)}, f32[1024,1024]{1,0:T(8,128)}) custom-call(bf16[512,1024]{1,0:T(8,128)(2,1)} %visits.1, bf16[1024,1024]{1,0:T(8,128)(2,1)} %weight.1, bf16[32,1024]{1,0:T(8,128)(2,1)} %table.1, s32[512,32]{1,0:T(8,128)} %copy.7.labels, s32[32,128]{1,0:T(8,128)} %bitcast.1), custom_call_target="tpu_custom_call" | custom-call | tf_op jit(solution)/shard_map/step/pallas_call | solution.py:458
  105.2 1.6 %copy.10 = f32[32,1024]{1,0:T(8,128)} copy(f32[32,1024]{1,0:T(8,128)} %get-tuple-element.4) | data formatting | bytes 262144
  106.8 4.8 %copy.11 = f32[1024,1024]{1,0:T(8,128)} copy(f32[1024,1024]{1,0:T(8,128)} %get-tuple-element.5) | data formatting | bytes 8388608

commit v2 on v1

v2 whole, which is shorter than its diff:
```python
import math

import jax
import jax.numpy as jnp
from jax import lax
from jax.experimental import pallas as pl
from jax.experimental.pallas import tpu as pltpu
from jax.sharding import PartitionSpec as P

MESH = pl.DeviceIdType.MESH
F32 = jnp.float32
BF16 = jnp.bfloat16
NN = (((1,), (0,)), ((), ()))
NT = (((1,), (1,)), ((), ()))

PARTS = ((0, 1, 2), (2, 1, 0), (2, 0, 1))
COLS = ((0, 384), (384, 384), (768, 256))
OFFS = (1, -1, 2)
REL = (0, 1, -1, 2)


def mod4(v):
    return lax.rem(v + 8, 4)


def kernel(
    visits, weight, table, labels, order, dgrad, wgrad,
    vis, vis_t, w_half, w_t, own_order, own_labels, order_t, sel, lab, coded, squash, tab, tab_t, res,
    cg_out, cg_in, cg_own, hgrad,
    s0, s1, s2, fp0, fp1, fp2, own0, own1, own2, hb0, hb1, hb2, rb0, rb1, rb2,
    r2a0, r2a1, r2a2, r2b0, r2b1, r2b2, r2s0, r2s1, r2s2,
    r3b0, r3b1, r3b2,
    wfull, wlow, w1b0, w1b1, w1b2, wp0, wp1, wp2, w2b0, w2b1, w2b2, wq0, wq1, wq2, w3b0, w3b1, w3b2, wout,
    load_sem, ag_s, ag_r, rs_s, rs_r, wt_s, wt_r, d2d_s, d2d_r, out_sem,
):
    g, i = lax.axis_index("group"), lax.axis_index("inner")
    x = (i // 8) * 2 + g // 4
    y = lax.rem(g, 4)
    z = lax.rem(i // 2, 4)
    core = lax.rem(i, 2)
    pos = (x, y, z)

    def device(px, py, pz, pc):
        return (lax.rem(px, 2) * 4 + py, (px // 2) * 8 + pz * 2 + pc)

    def peer(axis, off):
        moved = [mod4(v + off) if k == axis else v for k, v in enumerate(pos)]
        return device(*moved, core)

    sibling = device(x, y, z, 1 - core)
    def send(src, dst, ssem, rsem, to):
        copy = pltpu.make_async_remote_copy(
            src_ref=src, dst_ref=dst, send_sem=ssem, recv_sem=rsem, device_id=to, device_id_type=MESH
        )
        copy.start()

    def received(dst, rsem):
        pltpu.make_async_copy(dst, dst, rsem).wait()

    def cols(p):
        return pl.ds(COLS[p][0], COLS[p][1])

    def row_of(buf, p, b_at, c_at):
        a, b, c = PARTS[p]
        at = [None, None, None]
        at[a], at[b], at[c] = slice(None), b_at, c_at
        return buf.at[at[2], at[1], at[0], :, cols(p)]

    def block_of(buf, p, a_at, b_at, c_at):
        a, b, c = PARTS[p]
        at = [None, None, None]
        at[a], at[b], at[c] = a_at, b_at, c_at
        return buf.at[at[2], at[1], at[0], :, cols(p)]

    def plane_row(buf, p, b_at):
        return buf.at[b_at] if p == 0 else buf.at[:, b_at]

    mine = pl.ds(pl.multiple_of(core * 512, 512), 512)
    theirs = pl.ds(pl.multiple_of((1 - core) * 512, 512), 512)
    loads = [
        pltpu.make_async_copy(table, tab.at[z, y, x], load_sem.at[0]),
        pltpu.make_async_copy(weight.at[:, mine], w_half, load_sem.at[1]),
        pltpu.make_async_copy(visits, vis.at[mine], load_sem.at[2]),
        pltpu.make_async_copy(labels, own_labels, load_sem.at[3]),
        pltpu.make_async_copy(order, own_order, load_sem.at[4]),
    ]
    for load in loads:
        load.start()
    barrier = pltpu.get_barrier_semaphore()
    partners = [peer(axis, off) for axis in range(3) for off in OFFS] + [sibling]
    for partner in partners:
        pl.semaphore_signal(barrier, inc=1, device_id=partner, device_id_type=MESH)
    pl.semaphore_wait(barrier, len(partners))

    for k, off in enumerate(OFFS):
        for p in range(3):
            a, b, c = PARTS[p]
            send(table.at[:, cols(p)], block_of(tab, p, pos[a], pos[b], pos[c]), ag_s.at[p], ag_r.at[p, 15], peer(a, off))
    send(visits, vis.at[mine], d2d_s.at[0], d2d_r.at[0], sibling)

    loads[3].wait()
    column = lax.broadcasted_iota(jnp.int32, (32, 512), 0)
    ids_in_range = (own_labels[...] - column * 128).astype(F32)
    lab[mine, :] = jnp.concatenate([ids_in_range, jnp.ones((1, 512), F32), jnp.zeros((95, 512), F32)], axis=0).T.astype(BF16)
    send(lab.at[mine], lab.at[mine], d2d_s.at[1], d2d_r.at[1], sibling)
    loads[1].wait()
    w_t[...] = w_half[...].T
    loads[0].wait()
    for p in range(3):
        a, b, c = PARTS[p]
        received(block_of(tab, p, slice(0, 3), pos[b], pos[c]), ag_r.at[p, 15])

    def send_row_c(p, j, b_at):
        a, b, c = PARTS[p]
        row = row_of(tab, p, b_at, pos[c])
        for d, off in enumerate((1, -1)):
            send(row, row, ag_s.at[p], ag_r.at[p, 3 + 2 * j + d], peer(c, off))

    for p in range(3):
        a, b, c = PARTS[p]
        row = row_of(tab, p, pos[b], pos[c])
        for k, off in enumerate(OFFS):
            send(row, row, ag_s.at[p], ag_r.at[p, k], peer(b, off))
        send_row_c(p, 0, pos[b])

    def hidden_of(rows):
        hidden = lax.dot_general(w_t[...], vis[rows, :], NT, preferred_element_type=F32)
        value = jnp.tanh(hidden)
        squash[:, rows] = value
        coded[mine, rows] = value.astype(BF16)

    loads[2].wait()
    hidden_of(mine)

    for k, off in enumerate(OFFS):
        for p in range(3):
            a, b, c = PARTS[p]
            b_at = mod4(pos[b] - off)
            received(row_of(tab, p, b_at, pos[c]), ag_r.at[p, k])
            send_row_c(p, REL.index(-off if off != 2 else 2), b_at)

    received(vis.at[theirs], d2d_r.at[0])
    hidden_of(theirs)
    send(coded.at[mine], coded.at[mine], d2d_s.at[2], d2d_r.at[2], sibling)

    def take_row(j):
        for p in range(3):
            a, b, c = PARTS[p]
            b_at = mod4(pos[b] + REL[j])
            low = row_of(tab, p, b_at, mod4(pos[c] - 1))
            received(low, ag_r.at[p, 3 + 2 * j])
            if j in (0, 1):
                send(low, low, ag_s.at[p], ag_r.at[p, 11 + j], peer(c, 1))
            high = row_of(tab, p, b_at, mod4(pos[c] + 1))
            received(high, ag_r.at[p, 4 + 2 * j])
            if j in (2, 3):
                send(high, high, ag_s.at[p], ag_r.at[p, 11 + j], peer(c, -1))

    take_row(0)
    loads[4].wait()
    order_t[...] = own_order[...].astype(F32).T
    lane_q = lax.broadcasted_iota(jnp.int32, (32, 32), 1)
    lane_j = lax.broadcasted_iota(jnp.int32, (32, 128), 1)

    def select(n, _):
        bz, by, bx = n // 16, lax.rem(n // 4, 4), lax.rem(n, 4)
        q = (lax.rem(bx, 2) * 4 + by) * 4 + (bx // 2) * 2 + bz // 2
        m = lax.rem(bz, 2) * 2 + core
        rows = order_t[pl.ds(pl.multiple_of(m * 32, 32), 32), :]
        ids = jnp.sum(jnp.where(lane_q == q, rows, 0.0), axis=1, keepdims=True).astype(jnp.int32)
        ids = jnp.broadcast_to(ids, (32, 128))
        picked = jnp.where(lane_j == (ids >> 7), 1.0, 0.0)
        sel[n] = jnp.where(lane_j == 32, -(ids & 127).astype(F32), picked).astype(BF16)
        return 0

    lax.fori_loop(0, 64, select, 0)
    take_row(2)
    vis_t[...] = vis[...].T
    take_row(1)
    take_row(3)
    received(coded.at[theirs], d2d_r.at[2])
    received(lab.at[theirs], d2d_r.at[1])
    for j in (0, 1, 2, 3):
        for p in range(3):
            a, b, c = PARTS[p]
            row = row_of(tab, p, mod4(pos[b] + REL[j]), mod4(pos[c] + 2))
            received(row, ag_r.at[p, 11 + j])

    scale = 1.0 / 256.0

    def residual_of(plane, _):
        rows = tab[plane].reshape(512, 1024)
        picks = sel[pl.ds(plane * 16, 16)].reshape(512, 128)
        for half in range(2):
            seen = pl.ds(half * 512, 512)
            logits = lax.dot_general(rows, coded[:, seen], NN, preferred_element_type=F32)
            gap = lax.dot_general(picks, lab[seen, :], NT, preferred_element_type=F32)
            prob = 0.5 * jnp.tanh(0.5 * logits) + 0.5
            value = (prob - jnp.where(gap == 0.0, 1.0, 0.0)) * scale
            res[plane, :, :, :, seen] = value.astype(BF16).reshape(4, 4, 32, 512)
        tab_t[:, pl.ds(pl.multiple_of(plane * 512, 512), 512)] = rows.T
        return 0

    lax.fori_loop(0, 4, residual_of, 0)

    flat = res.reshape(2048, 1024)

    def coded_grad(at):
        rows = tab_t[pl.ds(pl.multiple_of(at, 128), 128), :]
        return lax.dot_general(rows, flat[...], NN, preferred_element_type=F32)

    def away(n, _):
        part = pl.ds(pl.multiple_of(n * 128, 128), 128)
        cg_out[part, :] = coded_grad((1 - core) * 512 + n * 128).astype(BF16)
        send(cg_out.at[part], cg_in.at[part], d2d_s.at[3], d2d_r.at[3], sibling)
        return 0

    lax.fori_loop(0, 4, away, 0)

    s, fp, own = (s0, s1, s2), (fp0, fp1, fp2), (own0, own1, own2)
    hb, rb = (hb0, hb1, hb2), (rb0, rb1, rb2)
    r2a, r2b, r2s, r3b = (r2a0, r2a1, r2a2), (r2b0, r2b1, r2b2), (r2s0, r2s1, r2s2), (r3b0, r3b1, r3b2)

    def term(p, off):
        c_at = mod4(pos[PARTS[p][2]] + off)
        rows = (res[c_at], res[:, :, c_at], res[:, c_at])[p].reshape(512, 1024)
        value = lax.dot_general(rows, coded[cols(p), :], NT, preferred_element_type=F32)
        return value.reshape(4, 4, 32, COLS[p][1])

    for p in range(3):
        a, b, c = PARTS[p]
        s[p][2] = term(p, 2).astype(BF16)
        for j in range(4):
            src = plane_row(s[p].at[2], p, mod4(pos[b] + REL[j]))
            send(src, hb[p].at[j], rs_s.at[p, 0], rs_r.at[p, j], peer(c, 1 if j < 2 else -1))

    def home(n, _):
        cg_own[pl.ds(pl.multiple_of(n * 128, 128), 128), :] = coded_grad(core * 512 + n * 128)
        return 0

    lax.fori_loop(0, 4, home, 0)
    received(cg_in, d2d_r.at[3])
    hgrad[...] = ((cg_own[...] + cg_in[...].astype(F32)) * (1.0 - squash[...] * squash[...])).astype(BF16)

    for half in range(2):
        value = lax.dot_general(vis_t[pl.ds(half * 512, 512), :], hgrad[...], NT, preferred_element_type=F32)
        wfull[:, pl.ds(half * 512, 512)] = value
        wlow[:, pl.ds(half * 512, 512)] = value.astype(BF16)
    w1b, wp, w2b, wq, w3b = (
        (w1b0, w1b1, w1b2), (wp0, wp1, wp2), (w2b0, w2b1, w2b2), (wq0, wq1, wq2), (w3b0, w3b1, w3b2)
    )

    def span(at, size):
        return pl.ds(pl.multiple_of(at * size, size), size)

    for k, off in enumerate(OFFS):
        for p in range(3):
            c = PARTS[p][2]
            src = wlow.at[span(mod4(pos[c] + off), 128), cols(p)]
            send(src, w1b[p].at[k], wt_s.at[p, 0], wt_r.at[p, 0], peer(c, off))

    def send_term_row(p, k, j):
        b, c = PARTS[p][1], PARTS[p][2]
        src = plane_row(s[p].at[k], p, mod4(pos[b] + REL[j]))
        send(src, rb[p].at[k, j], rs_s.at[p, 0], rs_r.at[p, 4 + 4 * k + j], peer(c, OFFS[k]))

    for k in range(2):
        for p in range(3):
            a, b, c = PARTS[p]
            value = term(p, OFFS[k])
            fp[p][k] = value
            s[p][k] = value.astype(BF16)
            for j in (2, 3) if k == 0 else (0, 1):
                send_term_row(p, k, j)

    for j in (0, 2, 1, 3):
        k = 0 if j < 2 else 1
        for p in range(3):
            a, b, c = PARTS[p]
            received(hb[p].at[j], rs_r.at[p, j])
            b_at = mod4(pos[b] + REL[j])
            whole = plane_row(fp[p].at[k], p, b_at)[...] + hb[p][j].astype(F32)
            plane_row(s[p].at[k], p, b_at)[...] = whole.astype(BF16)
            send_term_row(p, k, j)

    for p in range(3):
        c = PARTS[p][2]
        received(w1b[p], wt_r.at[p, 0])
        wp[p][...] = (
            wfull[span(pos[c], 128), cols(p)]
            + w1b[p][0].astype(F32) + w1b[p][1].astype(F32) + w1b[p][2].astype(F32)
        )
        b = PARTS[p][1]
        for k, off in enumerate(OFFS):
            src = wp[p].at[span(mod4(pos[b] + off), 32)]
            send(src, w2b[p].at[k], wt_s.at[p, 1], wt_r.at[p, 1], peer(b, off))

    for p in range(3):
        own[p][...] = term(p, 0)

    def sum_c(p):
        a, b, c = PARTS[p]
        for j in (2, 0, 1, 3):
            for k in range(2):
                received(rb[p].at[k, j], rs_r.at[p, 4 + 4 * k + j])
            mine_row = plane_row(own[p], p, mod4(pos[b] + REL[j]))
            mine_row[...] = mine_row[...] + rb[p][0, j].astype(F32) + rb[p][1, j].astype(F32)
        r2a[p][...] = own[p][...].astype(BF16)
        for k, off in enumerate(OFFS):
            src = plane_row(r2a[p], p, mod4(pos[b] + off))
            send(src, r2b[p].at[k], rs_s.at[p, 0], rs_r.at[p, 12], peer(b, off))

    for p in range(3):
        a, b, c = PARTS[p]
        received(w2b[p], wt_r.at[p, 1])
        wq[p][...] = wp[p][span(pos[b], 32), :] + w2b[p][0] + w2b[p][1] + w2b[p][2]
        for k, off in enumerate(OFFS):
            src = wq[p].at[span(mod4(pos[a] + off), 8)]
            send(src, w3b[p].at[k], wt_s.at[p, 1], wt_r.at[p, 2], peer(a, off))

    sum_c(0)

    for p in range(3):
        a, b, c = PARTS[p]
        received(w3b[p], wt_r.at[p, 2])
        at = span((pos[c] * 4 + pos[b]) * 4 + pos[a], 8)
        wout[at, cols(p)] = wq[p][span(pos[a], 8), :] + w3b[p][0] + w3b[p][1] + w3b[p][2]
        for k, off in enumerate(OFFS):
            block = wout.at[at, cols(p)]
            send(block, block, wt_s.at[p, 1], wt_r.at[p, 3], peer(a, off))

    sum_c(1)

    for p in range(3):
        a, b, c = PARTS[p]
        received(wout.at[pl.ds(0, 24), cols(p)], wt_r.at[p, 3])
        for k, off in enumerate(OFFS):
            row = wout.at[span(pos[c] * 4 + pos[b], 32), cols(p)]
            send(row, row, wt_s.at[p, 1], wt_r.at[p, 4], peer(b, off))

    sum_c(2)

    pieces = (((0, 0, 384),), ((384, 0, 128), (512, 1, 256)), ((768, 1, 256),))

    def deliver(p, c_at):
        for lo, half, size in pieces[p]:
            src = wout.at[span(c_at, 128), pl.ds(lo, size)]
            dst = wgrad.at[
                pl.ds(pl.multiple_of(half * 512 + c_at * 128, 128), 128),
                pl.ds(pl.multiple_of(core * 512 + lo - half * 512, 128), size),
            ]
            pltpu.make_async_copy(src, dst, out_sem.at[0]).start()
            send(src, dst, out_sem.at[1], out_sem.at[2], sibling)

    for p in range(3):
        a, b, c = PARTS[p]
        received(wout.at[pl.ds(0, 96), cols(p)], wt_r.at[p, 4])
        plane = wout.at[span(pos[c], 128), cols(p)]
        for k, off in enumerate((1, -1)):
            send(plane, plane, wt_s.at[p, 2], wt_r.at[p, 5 + k], peer(c, off))
        deliver(p, pos[c])

    for p in range(3):
        a, b, c = PARTS[p]
        received(r2b[p], rs_r.at[p, 12])
        r2s[p][...] = (
            plane_row(own[p], p, pos[b])[...] + r2b[p][0].astype(F32) + r2b[p][1].astype(F32) + r2b[p][2].astype(F32)
        )
        for k, off in enumerate(OFFS):
            send(r2s[p].at[mod4(pos[a] + off)], r3b[p].at[k], rs_s.at[p, 1], rs_r.at[p, 13], peer(a, off))

    for p in range(3):
        c = PARTS[p][2]
        for k, off in enumerate((1, -1)):
            at = mod4(pos[c] - off)
            received(wout.at[span(at, 128), cols(p)], wt_r.at[p, 5 + k])
            half = wout.at[span(at * 2 + k, 64), cols(p)]
            send(half, half, wt_s.at[p, 2], wt_r.at[p, 7 + k], peer(c, off))
            deliver(p, at)

    for p in range(3):
        a, b, c = PARTS[p]
        received(r3b[p], rs_r.at[p, 13])
        dgrad[:, cols(p)] = r2s[p][pos[a]] + r3b[p][0] + r3b[p][1] + r3b[p][2]

    for p in range(3):
        c = PARTS[p][2]
        at = mod4(pos[c] + 2)
        for k in range(2):
            received(wout.at[span(at * 2 + k, 64), cols(p)], wt_r.at[p, 7 + k])
        deliver(p, at)

    flat_tab = tab.reshape(64, 32, 1024)
    for p in range(3):
        received(flat_tab.at[pl.ds(0, 63), :, cols(p)], ag_s.at[p])
        received(flat_tab.at[pl.ds(0, 60), :, cols(p)], rs_s.at[p, 0])
        received(r3b[p], rs_s.at[p, 1])
        received(w1b[p], wt_s.at[p, 0])
        received(wout.at[pl.ds(0, 240), cols(p)], wt_s.at[p, 1])
        received(wout.at[pl.ds(0, 384), cols(p)], wt_s.at[p, 2])
    for n, ref in enumerate((vis.at[mine], lab.at[mine], coded.at[mine], cg_out)):
        received(ref, d2d_s.at[n])
    for n in range(3):
        received(wout, out_sem.at[n])


def per_part(make):
    return [make(width) for _, width in COLS]


def local(visits, enc_weight, drug_table, labels, drug_order):
    vmem = pltpu.VMEM
    scratch = [
        vmem((1024, 1024), BF16), vmem((1024, 1024), BF16), vmem((1024, 512), BF16), vmem((512, 1024), BF16),
        vmem((32, 128), jnp.int32), vmem((32, 512), jnp.int32), vmem((128, 32), F32),
        vmem((64, 32, 128), BF16), vmem((1024, 128), BF16), vmem((1024, 1024), BF16), vmem((512, 1024), F32),
        vmem((4, 4, 4, 32, 1024), BF16), vmem((1024, 2048), BF16), vmem((4, 4, 4, 32, 1024), BF16),
        vmem((512, 1024), BF16), vmem((512, 1024), BF16), vmem((512, 1024), F32), vmem((512, 1024), BF16),
        *per_part(lambda n: vmem((3, 4, 4, 32, n), BF16)),
        *per_part(lambda n: vmem((2, 4, 4, 32, n), F32)),
        *per_part(lambda n: vmem((4, 4, 32, n), F32)),
        *per_part(lambda n: vmem((4, 4, 32, n), BF16)),
        *per_part(lambda n: vmem((2, 4, 4, 32, n), BF16)),
        *per_part(lambda n: vmem((4, 4, 32, n), BF16)),
        *per_part(lambda n: vmem((3, 4, 32, n), BF16)),
        *per_part(lambda n: vmem((4, 32, n), F32)),
        *per_part(lambda n: vmem((3, 32, n), F32)),
        vmem((512, 1024), F32), vmem((512, 1024), BF16),
        *per_part(lambda n: vmem((3, 128, n), BF16)),
        *per_part(lambda n: vmem((128, n), F32)),
        *per_part(lambda n: vmem((3, 32, n), F32)),
        *per_part(lambda n: vmem((32, n), F32)),
        *per_part(lambda n: vmem((3, 8, n), F32)),
        vmem((512, 1024), F32),
        pltpu.SemaphoreType.DMA((5,)),
        pltpu.SemaphoreType.DMA((3,)), pltpu.SemaphoreType.DMA((3, 16)),
        pltpu.SemaphoreType.DMA((3, 2)), pltpu.SemaphoreType.DMA((3, 14)),
        pltpu.SemaphoreType.DMA((3, 3)), pltpu.SemaphoreType.DMA((3, 9)),
        pltpu.SemaphoreType.DMA((4,)), pltpu.SemaphoreType.DMA((4,)), pltpu.SemaphoreType.DMA((3,)),
    ]
    anywhere = pl.BlockSpec(memory_space=pl.ANY)
    return pl.pallas_call(
        kernel,
        name="step",
        out_shape=(jax.ShapeDtypeStruct((32, 1024), F32), jax.ShapeDtypeStruct((1024, 1024), F32)),
        in_specs=[anywhere] * 5,
        out_specs=(pl.BlockSpec(memory_space=pltpu.VMEM), anywhere),
        scratch_shapes=scratch,
        compiler_params=pltpu.CompilerParams(
            collective_id=0, has_side_effects=True, vmem_limit_bytes=60 * 2**20
        ),
    )(visits, enc_weight, drug_table, labels.T, drug_order.reshape(32, 128))


def solution(mesh):
    return jax.shard_map(
        local,
        mesh=mesh,
        in_specs=(
            P(("group", "inner"), None),
            P(),
            P(("group", "inner"), None),
            P(("group", "inner"), None),
            P(),
        ),
        out_specs=(P(("group", "inner"), None), P()),
        check_vma=False,
    )
```

time: 112 us -> 101 us (0.902)
  Pallas kernels: 103 us -> 94.1 us
  local copies, waits for them, and re-layouts: 8.03 us -> 6.36 us
    pallas_call x1, Pallas kernels: 103 us -> 94.1 us  [local(): pl.pallas_call(kernel, name='step', out_shape=(jax.ShapeDtypeStruct((32,...]
    unnamed x3 -> x2, local copies, waits for them, and re-layouts: 8.03 us -> 6.36 us
where the time goes in v2:
time: 101 us
  Pallas kernels  94.1 us (93%)
  local copies, waits for them, and re-layouts  6.36 us (6%)
    pallas_call x1, Pallas kernels, local(): pl.pallas_call(kernel, name='step', out_shape=(jax.ShapeDtypeStruct((32,...  94.1 us
    unnamed x2, local copies, waits for them, and re-layouts  6.36 us

profile of v2, /device:TPU:1, one launch (start us, length us, event | category | flops | bytes accessed | tf_op | source)
XLA Modules:
  0.0 101.1 jit_solution(11172988419163906146)
XLA Ops:
  0.6 94.1 %step.1 = (f32[32,1024]{1,0:T(8,128)}, f32[1024,1024]{1,0:T(8,128)}) custom-call(bf16[512,1024]{1,0:T(8,128)(2,1)} %visits.1, bf16[1024,1024]{1,0:T(8,128)(2,1)} %weight.1, bf16[32,1024]{1,0:T(8,128)(2,1)} %table.1, s32[32,512]{1,0:T(8,128)} %bitcast.2, s32[32,128]{1,0:T(8,128)} %bitcast.3), custom_call_target="tpu_custom_call" | custom-call | tf_op jit(solution)/shard_map/step/pallas_call | solution.py:442
  94.8 1.6 %copy.9 = f32[32,1024]{1,0:T(8,128)} copy(f32[32,1024]{1,0:T(8,128)} %get-tuple-element.4) | data formatting | bytes 262144
  96.3 4.8 %copy.10 = f32[1024,1024]{1,0:T(8,128)} copy(f32[1024,1024]{1,0:T(8,128)} %get-tuple-element.5) | data formatting | bytes 8388608

commit v3 on v0

v3 whole, which is shorter than its diff:
```python
import math

import jax
import jax.numpy as jnp
from jax import lax
from jax.experimental import pallas as pl
from jax.experimental.pallas import tpu as pltpu
from jax.sharding import PartitionSpec as P

MESH = pl.DeviceIdType.MESH
F32 = jnp.float32
BF16 = jnp.bfloat16
NN = (((1,), (0,)), ((), ()))
NT = (((1,), (1,)), ((), ()))

PARTS = ((0, 1, 2), (1, 2, 0), (2, 0, 1))
COLS = ((0, 384), (384, 384), (768, 256))
OFFS = (1, -1, 2)
REL = (0, 1, -1, 2)
BACK = {1: 2, -1: 1, 2: 3}


def mod4(v):
    return lax.rem(v + 8, 4)


def kernel(
    visits, weight, table, labels, order, dgrad, wgrad,
    vis, vis_t, w_half, w_t, own_order, own_labels, order_t, sel, lab, coded, squash, tab, tab_t, res,
    cg_out, cg_in, cg_own, hgrad,
    s0, s1, s2, fp0, fp1, fp2, own0, own1, own2, hb0, hb1, hb2, rb0, rb1, rb2,
    r2a0, r2a1, r2a2, r2b0, r2b1, r2b2, r2s0, r2s1, r2s2,
    r3b0, r3b1, r3b2,
    wfull, wlow, w1b0, w1b1, w1b2, wp0, wp1, wp2, w2b0, w2b1, w2b2, w3b0, w3b1, w3b2, wout,
    load_sem, ag_s, ag_r, rs_s, rs_r, wt_s, wt_r, d2d_s, d2d_r, out_sem,
):
    g, i = lax.axis_index("group"), lax.axis_index("inner")
    x = (i // 8) * 2 + g // 4
    y = lax.rem(g, 4)
    z = lax.rem(i // 2, 4)
    core = lax.rem(i, 2)
    pos = (x, y, z)

    def device(px, py, pz, pc):
        return (lax.rem(px, 2) * 4 + py, (px // 2) * 8 + pz * 2 + pc)

    def peer_of(axis, off):
        moved = [mod4(v + off) if k == axis else v for k, v in enumerate(pos)]
        return device(*moved, core)

    peers = {(axis, off): peer_of(axis, off) for axis in range(3) for off in OFFS}

    def peer(axis, off):
        return peers[axis, off]

    places = {(axis, off): mod4(pos[axis] + off) if off else pos[axis] for axis in range(3) for off in REL}
    sibling = device(x, y, z, 1 - core)
    def send(src, dst, ssem, rsem, to):
        copy = pltpu.make_async_remote_copy(
            src_ref=src, dst_ref=dst, send_sem=ssem, recv_sem=rsem, device_id=to, device_id_type=MESH
        )
        copy.start()

    def received(dst, rsem):
        pltpu.make_async_copy(dst, dst, rsem).wait()

    def cols(p):
        return pl.ds(COLS[p][0], COLS[p][1])

    def row_of(buf, p, b_at, c_at, a_at=slice(None)):
        a, b, c = PARTS[p]
        at = [None, None, None]
        at[a], at[b], at[c] = a_at, b_at, c_at
        return buf.at[at[2], at[1], at[0], :, cols(p)]

    def plane_row(buf, p, b_at):
        return buf.at[:, b_at] if p == 2 else buf.at[b_at]

    mine = pl.ds(pl.multiple_of(core * 512, 512), 512)
    theirs = pl.ds(pl.multiple_of((1 - core) * 512, 512), 512)
    loads = [
        pltpu.make_async_copy(table, tab.at[0, 0, 0], load_sem.at[0]),
        pltpu.make_async_copy(weight.at[:, mine], w_half, load_sem.at[1]),
        pltpu.make_async_copy(visits, vis.at[mine], load_sem.at[2]),
        pltpu.make_async_copy(labels, own_labels, load_sem.at[3]),
        pltpu.make_async_copy(order, own_order, load_sem.at[4]),
    ]
    for load in loads:
        load.start()
    barrier = pltpu.get_barrier_semaphore()
    partners = [peer(axis, off) for axis in range(3) for off in OFFS] + [sibling]
    for partner in partners:
        pl.semaphore_signal(barrier, inc=1, device_id=partner, device_id_type=MESH)
    pl.semaphore_wait(barrier, len(partners))

    def own_block():
        for off in OFFS:
            for p in range(3):
                a, b, c = PARTS[p]
                send(table.at[:, cols(p)], row_of(tab, p, 0, 0, BACK[off]), ag_s.at[p], ag_r.at[p, 15], peer(a, off))

    def send_row_c(p, j):
        for d, off in enumerate((1, -1)):
            to = row_of(tab, p, j, BACK[off])
            send(row_of(tab, p, j, 0), to, ag_s.at[p], ag_r.at[p, 3 + 2 * j + d], peer(PARTS[p][2], off))

    def own_row():
        loads[0].wait()
        for p in range(3):
            received(row_of(tab, p, 0, 0, slice(1, 4)), ag_r.at[p, 15])
        for p in range(3):
            for k, off in enumerate(OFFS):
                to = row_of(tab, p, BACK[off], 0)
                send(row_of(tab, p, 0, 0), to, ag_s.at[p], ag_r.at[p, k], peer(PARTS[p][1], off))
            send_row_c(p, 0)

    def rows_of_b():
        for k, off in enumerate(OFFS):
            for p in range(3):
                received(row_of(tab, p, BACK[off], 0), ag_r.at[p, k])
                send_row_c(p, BACK[off])

    def rows_of_c(j):
        for p in range(3):
            for d, off in enumerate((1, -1)):
                row = row_of(tab, p, j, BACK[off])
                received(row, ag_r.at[p, 3 + 2 * j + d])
                if (j in (0, 1)) == (d == 0):
                    send(row, row_of(tab, p, j, 3), ag_s.at[p], ag_r.at[p, 11 + j], peer(PARTS[p][2], off))

    def far_rows():
        for j in range(4):
            for p in range(3):
                received(row_of(tab, p, j, 3), ag_r.at[p, 11 + j])

    def hidden_of(rows):
        hidden = lax.dot_general(w_t[...], vis[rows, :], NT, preferred_element_type=F32)
        value = jnp.tanh(hidden)
        squash[:, rows] = value
        coded[mine, rows] = value.astype(BF16)

    lane_q = lax.broadcasted_iota(jnp.int32, (32, 32), 1)
    lane_j = lax.broadcasted_iota(jnp.int32, (32, 128), 1)

    def away_by(v, at):
        return lax.rem(v + at + jnp.where(at == 2, 1, 0) - jnp.where(at == 3, 1, 0), 4)

    def select(n, _):
        bz, by, bx = away_by(z, n // 16), away_by(y, lax.rem(n // 4, 4)), away_by(x, lax.rem(n, 4))
        q = (lax.rem(bx, 2) * 4 + by) * 4 + (bx // 2) * 2 + bz // 2
        m = lax.rem(bz, 2) * 2 + core
        rows = order_t[pl.ds(pl.multiple_of(m * 32, 32), 32), :]
        ids = jnp.sum(jnp.where(lane_q == q, rows, 0.0), axis=1, keepdims=True).astype(jnp.int32)
        ids = jnp.broadcast_to(ids, (32, 128))
        picked = jnp.where(lane_j == (ids >> 7), 1.0, 0.0)
        sel[n // 16, lax.rem(n // 4, 4), lax.rem(n, 4)] = jnp.where(lane_j == 32, -(ids & 127).astype(F32), picked).astype(BF16)
        return 0

    scale = 1.0 / 256.0

    def residual_of(zs, ys, xs):
        shape = tuple(v.stop - v.start for v in (zs, ys, xs))
        count = shape[0] * shape[1] * shape[2] * 32
        rows = tab[zs, ys, xs].reshape(count, 1024)
        picks = sel[zs, ys, xs].reshape(count, 128)
        for half in range(2):
            seen = pl.ds(half * 512, 512)
            logits = lax.dot_general(rows, coded[:, seen], NN, preferred_element_type=F32)
            gap = lax.dot_general(picks, lab[seen, :], NT, preferred_element_type=F32)
            prob = 0.5 * jnp.tanh(0.5 * logits) + 0.5
            value = (prob - jnp.where(gap == 0.0, 1.0, 0.0)) * scale
            res[zs, ys, xs, :, seen] = value.astype(BF16).reshape(*shape, 32, 512)

    def turn(n, _):
        tab_t[:, pl.ds(pl.multiple_of(n * 512, 512), 512)] = tab[n].reshape(512, 1024).T
        return 0

    near, far, all_of = slice(0, 3), slice(3, 4), slice(0, 4)

    own_block()
    send(visits, vis.at[mine], d2d_s.at[0], d2d_r.at[0], sibling)
    loads[3].wait()
    column = lax.broadcasted_iota(jnp.int32, (32, 512), 0)
    ids_in_range = (own_labels[...] - column * 128).astype(F32)
    lab[mine, :] = jnp.concatenate([ids_in_range, jnp.ones((1, 512), F32), jnp.zeros((95, 512), F32)], axis=0).T.astype(BF16)
    send(lab.at[mine], lab.at[mine], d2d_s.at[1], d2d_r.at[1], sibling)
    own_row()
    loads[1].wait()
    w_t[...] = w_half[...].T
    loads[2].wait()
    hidden_of(mine)
    rows_of_b()
    received(vis.at[theirs], d2d_r.at[0])
    hidden_of(theirs)
    send(coded.at[mine], coded.at[mine], d2d_s.at[2], d2d_r.at[2], sibling)
    rows_of_c(0)
    loads[4].wait()
    order_t[...] = own_order[...].astype(F32).T
    lax.fori_loop(0, 64, select, 0)
    rows_of_c(2)
    vis_t[...] = vis[...].T
    rows_of_c(1)
    rows_of_c(3)
    received(coded.at[theirs], d2d_r.at[2])
    received(lab.at[theirs], d2d_r.at[1])

    for n in range(3):
        residual_of(slice(n, n + 1), near, near)
    far_rows()
    residual_of(far, all_of, all_of)
    residual_of(near, far, all_of)
    residual_of(near, near, far)
    lax.fori_loop(0, 4, turn, 0)

    flat = res.reshape(2048, 1024)

    def coded_grad(at):
        rows = tab_t[pl.ds(pl.multiple_of(at, 128), 128), :]
        return lax.dot_general(rows, flat[...], NN, preferred_element_type=F32)

    def away(n, _):
        part = pl.ds(pl.multiple_of(n * 128, 128), 128)
        cg_out[part, :] = coded_grad((1 - core) * 512 + n * 128).astype(BF16)
        send(cg_out.at[part], cg_in.at[part], d2d_s.at[3], d2d_r.at[3], sibling)
        return 0

    lax.fori_loop(0, 4, away, 0)

    s, fp, own = (s0, s1, s2), (fp0, fp1, fp2), (own0, own1, own2)
    hb, rb = (hb0, hb1, hb2), (rb0, rb1, rb2)
    r2a, r2b, r2s, r3b = (r2a0, r2a1, r2a2), (r2b0, r2b1, r2b2), (r2s0, r2s1, r2s2), (r3b0, r3b1, r3b2)

    def term(p, at):
        rows = (res[at], res[:, :, at], res[:, at])[p].reshape(512, 1024)
        value = lax.dot_general(rows, coded[cols(p), :], NT, preferred_element_type=F32)
        return value.reshape(4, 4, 32, COLS[p][1])

    for p in range(3):
        s[p][2] = term(p, 3).astype(BF16)
        for j in range(4):
            src = plane_row(s[p].at[2], p, j)
            send(src, hb[p].at[j], rs_s.at[p, 0], rs_r.at[p, j], peer(PARTS[p][2], 1 if j < 2 else -1))

    def home(n, _):
        cg_own[pl.ds(pl.multiple_of(n * 128, 128), 128), :] = coded_grad(core * 512 + n * 128)
        return 0

    lax.fori_loop(0, 4, home, 0)
    received(cg_in, d2d_r.at[3])
    hgrad[...] = ((cg_own[...] + cg_in[...].astype(F32)) * (1.0 - squash[...] * squash[...])).astype(BF16)

    for half in range(2):
        value = lax.dot_general(vis_t[pl.ds(half * 512, 512), :], hgrad[...], NT, preferred_element_type=F32)
        wfull[:, pl.ds(half * 512, 512)] = value
        wlow[:, pl.ds(half * 512, 512)] = value.astype(BF16)
    w1b, wp, w2b, w3b = (w1b0, w1b1, w1b2), (wp0, wp1, wp2), (w2b0, w2b1, w2b2), (w3b0, w3b1, w3b2)

    def span(at, size):
        return pl.ds(pl.multiple_of(at * size, size), size)

    def w_row(c_at, b_at):
        return span(c_at * 4 + b_at, 32)

    for j in (1, 2, 3, 0):
        for k, off in enumerate(OFFS):
            for p in range(3):
                a, b, c = PARTS[p]
                src = wlow.at[w_row(places[c, off], places[b, REL[j]]), cols(p)]
                send(src, w1b[p].at[j, k], wt_s.at[p, 0], wt_r.at[p, j], peer(c, off))

    def w_sum_c():
        for j in (1, 2, 3, 0):
            for p in range(3):
                a, b, c = PARTS[p]
                received(w1b[p].at[j], wt_r.at[p, j])
                wp[p][j] = (
                    wfull[w_row(pos[c], places[b, REL[j]]), cols(p)]
                    + w1b[p][j, 0].astype(F32) + w1b[p][j, 1].astype(F32) + w1b[p][j, 2].astype(F32)
                )
                if j:
                    send(wp[p].at[j], w2b[p].at[j - 1], wt_s.at[p, 1], wt_r.at[p, 4], peer(b, REL[j]))

    def w_sum_b():
        for p in range(3):
            a, b, c = PARTS[p]
            received(w2b[p], wt_r.at[p, 4])
            w3b[p][pos[a]] = wp[p][0] + w2b[p][0] + w2b[p][1] + w2b[p][2]
            own_slot = w3b[p].at[pos[a]]
            for off in OFFS:
                send(own_slot, own_slot, wt_s.at[p, 1], wt_r.at[p, 5], peer(a, off))

    def w_send_c(p, j):
        a, b, c = PARTS[p]
        row = wout.at[w_row(0, places[b, REL[j]]), cols(p)]
        for d, off in enumerate((1, -1)):
            send(row, wout.at[w_row(BACK[off], places[b, REL[j]]), cols(p)], wt_s.at[p, 2], wt_r.at[p, 9 + 2 * j + d], peer(c, off))

    def w_sum_a():
        for p in range(3):
            a, b, c = PARTS[p]
            received(w3b[p].at[pl.ds(0, 3)], wt_r.at[p, 5])
            at = w_row(0, pos[b])
            wout[at, cols(p)] = w3b[p][0] + w3b[p][1] + w3b[p][2] + w3b[p][3]
            row = wout.at[at, cols(p)]
            for k, off in enumerate(OFFS):
                send(row, row, wt_s.at[p, 2], wt_r.at[p, 6 + k], peer(b, off))
            w_send_c(p, 0)

    pieces = (((0, 0, 384),), ((384, 0, 128), (512, 1, 256)), ((768, 1, 256),))

    def deliver(p, at):
        c_at = places[PARTS[p][2], REL[at]]
        for lo, half, size in pieces[p]:
            src = wout.at[pl.ds(at * 128, 128), pl.ds(lo, size)]
            dst = wgrad.at[
                pl.ds(pl.multiple_of(half * 512 + c_at * 128, 128), 128),
                pl.ds(pl.multiple_of(core * 512 + lo - half * 512, 128), size),
            ]
            pltpu.make_async_copy(src, dst, out_sem.at[0]).start()
            send(src, dst, out_sem.at[1], out_sem.at[2], sibling)

    def w_take_b():
        for k, off in enumerate(OFFS):
            for p in range(3):
                j = BACK[off]
                received(wout.at[w_row(0, places[PARTS[p][1], REL[j]]), cols(p)], wt_r.at[p, 6 + k])
                w_send_c(p, j)
        for p in range(3):
            deliver(p, 0)

    def w_take_c():
        for j in (0, 2, 1, 3):
            for p in range(3):
                a, b, c = PARTS[p]
                for d, off in enumerate((1, -1)):
                    row = wout.at[w_row(BACK[off], places[b, REL[j]]), cols(p)]
                    received(row, wt_r.at[p, 9 + 2 * j + d])
                    if (j in (0, 1)) == (d == 0):
                        to = wout.at[w_row(3, places[b, REL[j]]), cols(p)]
                        send(row, to, wt_s.at[p, 2], wt_r.at[p, 17 + j], peer(c, off))
        for p in range(3):
            deliver(p, 1)
            deliver(p, 2)

    def w_take_far():
        for p in range(3):
            for j in range(4):
                received(wout.at[w_row(3, places[PARTS[p][1], REL[j]]), cols(p)], wt_r.at[p, 17 + j])
            deliver(p, 3)

    def send_term_row(p, k, j):
        src = plane_row(s[p].at[k], p, j)
        send(src, rb[p].at[k, j], rs_s.at[p, 0], rs_r.at[p, 4 + 4 * k + j], peer(PARTS[p][2], OFFS[k]))

    def near_terms(k):
        for p in range(3):
            value = term(p, 1 + k)
            fp[p][k] = value
            s[p][k] = value.astype(BF16)
            for j in (2, 3) if k == 0 else (0, 1):
                send_term_row(p, k, j)

    def pass_on(j):
        k = 0 if j < 2 else 1
        for p in range(3):
            received(hb[p].at[j], rs_r.at[p, j])
            whole = plane_row(fp[p].at[k], p, j)[...] + hb[p][j].astype(F32)
            plane_row(s[p].at[k], p, j)[...] = whole.astype(BF16)
            send_term_row(p, k, j)

    def own_terms():
        for p in range(3):
            own[p][...] = term(p, 0)

    def sum_c(p):
        a, b, c = PARTS[p]
        for j in (2, 0, 1, 3):
            for k in range(2):
                received(rb[p].at[k, j], rs_r.at[p, 4 + 4 * k + j])
            mine_row = plane_row(own[p], p, j)
            mine_row[...] = mine_row[...] + rb[p][0, j].astype(F32) + rb[p][1, j].astype(F32)
        r2a[p][...] = own[p][...].astype(BF16)
        for k, off in enumerate(OFFS):
            src = plane_row(r2a[p], p, REL.index(off))
            send(src, r2b[p].at[k], rs_s.at[p, 0], rs_r.at[p, 12], peer(b, off))

    def sum_b():
        for p in range(3):
            a, b, c = PARTS[p]
            received(r2b[p], rs_r.at[p, 12])
            r2s[p][...] = (
                plane_row(own[p], p, 0)[...]
                + r2b[p][0].astype(F32) + r2b[p][1].astype(F32) + r2b[p][2].astype(F32)
            )
            for k, off in enumerate(OFFS):
                send(r2s[p].at[REL.index(off)], r3b[p].at[k], rs_s.at[p, 1], rs_r.at[p, 13], peer(a, off))

    def sum_a():
        for p in range(3):
            a, b, c = PARTS[p]
            received(r3b[p], rs_r.at[p, 13])
            dgrad[:, cols(p)] = r2s[p][0] + r3b[p][0] + r3b[p][1] + r3b[p][2]

    near_terms(0)
    near_terms(1)
    w_sum_c()
    own_terms()
    pass_on(0)
    pass_on(2)
    w_sum_b()
    pass_on(1)
    pass_on(3)
    w_sum_a()
    sum_c(0)
    w_take_b()
    sum_c(1)
    sum_c(2)
    w_take_c()
    sum_b()
    w_take_far()
    sum_a()

    flat_tab = tab.reshape(64, 32, 1024)
    for p in range(3):
        received(flat_tab.at[pl.ds(0, 63), :, cols(p)], ag_s.at[p])
        received(flat_tab.at[pl.ds(0, 60), :, cols(p)], rs_s.at[p, 0])
        received(r3b[p], rs_s.at[p, 1])
        received(w1b[p], wt_s.at[p, 0])
        received(wout.at[pl.ds(0, 192), cols(p)], wt_s.at[p, 1])
        received(wout.at[pl.ds(0, 480), cols(p)], wt_s.at[p, 2])
    for n, ref in enumerate((vis.at[mine], lab.at[mine], coded.at[mine], cg_out)):
        received(ref, d2d_s.at[n])
    for n in range(3):
        received(wout, out_sem.at[n])


def per_part(make):
    return [make(width) for _, width in COLS]


def local(visits, enc_weight, drug_table, labels, drug_order):
    vmem = pltpu.VMEM
    scratch = [
        vmem((1024, 1024), BF16), vmem((1024, 1024), BF16), vmem((1024, 512), BF16), vmem((512, 1024), BF16),
        vmem((32, 128), jnp.int32), vmem((32, 512), jnp.int32), vmem((128, 32), F32),
        vmem((4, 4, 4, 32, 128), BF16), vmem((1024, 128), BF16), vmem((1024, 1024), BF16), vmem((512, 1024), F32),
        vmem((4, 4, 4, 32, 1024), BF16), vmem((1024, 2048), BF16), vmem((4, 4, 4, 32, 1024), BF16),
        vmem((512, 1024), BF16), vmem((512, 1024), BF16), vmem((512, 1024), F32), vmem((512, 1024), BF16),
        *per_part(lambda n: vmem((3, 4, 4, 32, n), BF16)),
        *per_part(lambda n: vmem((2, 4, 4, 32, n), F32)),
        *per_part(lambda n: vmem((4, 4, 32, n), F32)),
        *per_part(lambda n: vmem((4, 4, 32, n), BF16)),
        *per_part(lambda n: vmem((2, 4, 4, 32, n), BF16)),
        *per_part(lambda n: vmem((4, 4, 32, n), BF16)),
        *per_part(lambda n: vmem((3, 4, 32, n), BF16)),
        *per_part(lambda n: vmem((4, 32, n), F32)),
        *per_part(lambda n: vmem((3, 32, n), F32)),
        vmem((512, 1024), F32), vmem((512, 1024), BF16),
        *per_part(lambda n: vmem((4, 3, 32, n), BF16)),
        *per_part(lambda n: vmem((4, 32, n), F32)),
        *per_part(lambda n: vmem((3, 32, n), F32)),
        *per_part(lambda n: vmem((4, 32, n), F32)),
        vmem((512, 1024), F32),
        pltpu.SemaphoreType.DMA((5,)),
        pltpu.SemaphoreType.DMA((3,)), pltpu.SemaphoreType.DMA((3, 16)),
        pltpu.SemaphoreType.DMA((3, 2)), pltpu.SemaphoreType.DMA((3, 14)),
        pltpu.SemaphoreType.DMA((3, 3)), pltpu.SemaphoreType.DMA((3, 21)),
        pltpu.SemaphoreType.DMA((4,)), pltpu.SemaphoreType.DMA((4,)), pltpu.SemaphoreType.DMA((3,)),
    ]
    anywhere = pl.BlockSpec(memory_space=pl.ANY)
    return pl.pallas_call(
        kernel,
        name="step",
        out_shape=(pltpu.VMEM((32, 1024), F32), pltpu.VMEM((1024, 1024), F32)),
        in_specs=[anywhere] * 5,
        out_specs=[pl.BlockSpec(memory_space=pltpu.VMEM)] * 2,
        scratch_shapes=scratch,
        compiler_params=pltpu.CompilerParams(
            collective_id=0, has_side_effects=True, vmem_limit_bytes=54 * 2**20
        ),
    )(visits, enc_weight, drug_table, labels.T, drug_order.reshape(32, 128))


def solution(mesh):
    return jax.shard_map(
        local,
        mesh=mesh,
        in_specs=(
            P(("group", "inner"), None),
            P(),
            P(("group", "inner"), None),
            P(("group", "inner"), None),
            P(),
        ),
        out_specs=(P(("group", "inner"), None), P()),
        check_vma=False,
    )
```

time: 655 us -> 87.7 us (0.13)
  waiting for transfers between devices: 526 us -> 0 us
  Pallas kernels: 0 us -> 83.9 us
  other arithmetic: 70.1 us -> 0 us
  matrix products: 34 us -> 0 us
  between operations: 13.8 us -> 0.64 us
  local copies, waits for them, and re-layouts: 9.29 us -> 2.67 us
    reduce_scatter x2 -> x0, waiting for transfers between devices: 223 us -> none  [the longest x1 156 us: local(): lax.psum_scatter(local_term(residual, coded), 'group', scatter_dimension=...]
    psum x1 -> x0, waiting for transfers between devices: 158 us -> none  [local(): weight_grad = lax.psum(weight_part, ('group', 'inner'))]
    all_gather x1 -> x0, waiting for transfers between devices: 144 us -> none  [local(): piece = lax.all_gather(drug_table, ('group', 'inner'), axis=0, tiled=True)]
    pallas_call x0 -> x1, Pallas kernels: none -> 83.9 us  [local(): pl.pallas_call(kernel, name='step', out_shape=(pltpu.VMEM((32, 1024), F32...]
    reduce_or x1 -> x0, other arithmetic: 58.8 us -> none  [local(): labelled = jnp.any(matches, axis=1).astype(jnp.float32)]
    dot_general x4 -> x0, matrix products: 34 us -> none  [the longest x1 12.7 us: local(): lax.dot_general(visits, hidden_grad, (((0,), (0,)), ((), ())), preferred_...]
    convert_element_type x1 -> x0, other arithmetic: 11.3 us -> none  [local_term(): lax.optimization_barrier(term.astype(jnp.bfloat16)).astype(jnp.float32)]
    unnamed x12 -> x2, local copies, waits for them, and re-layouts: 9.29 us -> 2.67 us
  transfers between devices with their start and end apart: 4 -> 0, of which waited for: 4 -> 0; matrix products, arithmetic and copies ran while one was open for 13% -> 0% of each run, Pallas kernels for 0% -> 0%
where the time goes in v3:
time: 87.7 us; the launch traced here: 87.2 us
  Pallas kernels  83.9 us (96%)
  local copies, waits for them, and re-layouts  2.67 us (3%)
    pallas_call x1, Pallas kernels, local(): pl.pallas_call(kernel, name='step', out_shape=(pltpu.VMEM((32, 1024), F32...  83.9 us
    unnamed x2, local copies, waits for them, and re-layouts  2.67 us

profile of v3, /device:TPU:1, one launch (start us, length us, event | category | flops | bytes accessed | tf_op | source)
XLA Modules:
  0.0 87.2 jit_solution(18369105463355988692)
XLA Ops:
  0.6 83.9 %step.1 = (f32[32,1024]{1,0:T(8,128)S(1)}, f32[1024,1024]{1,0:T(8,128)S(1)}) custom-call(bf16[512,1024]{1,0:T(8,128)(2,1)} %visits.1, bf16[1024,1024]{1,0:T(8,128)(2,1)} %weight.1, bf16[32,1024]{1,0:T(8,128)(2,1)} %table.1, s32[32,512]{1,0:T(8,128)} %bitcast.2, s32[32,128]{1,0:T(8,128)} %bitcast.3), custom_call_target="tpu_custom_call" | custom-call | tf_op jit(solution)/shard_map/step/pallas_call | solution.py:471
  84.5 0.7 copy.9
  85.2 2.0 %copy.10 = f32[1024,1024]{1,0:T(8,128)} copy(f32[1024,1024]{1,0:T(8,128)S(1)} %get-tuple-element.3) | data formatting | bytes 8388608

commit v4 on v3

--- a/solution.py
+++ b/solution.py
@@ -18,6 +18,22 @@
 OFFS = (1, -1, 2)
 REL = (0, 1, -1, 2)
 BACK = {1: 2, -1: 1, 2: 3}
+
+
+STEPS = 780.0
+FLOOR = 20.0
+
+
+def encode(value):
+    size = jnp.maximum(jnp.abs(value), 2.0**-FLOOR)
+    code = jnp.minimum(jnp.round((jnp.log2(size) + FLOOR) * STEPS), 32767.0)
+    return jnp.where(value < 0.0, -code, code).astype(jnp.int32).astype(jnp.int16)
+
+
+def decode(code):
+    code = code.astype(jnp.int32).astype(F32)
+    size = jnp.exp2(jnp.abs(code) * (1.0 / STEPS) - FLOOR)
+    return jnp.where(code == 0.0, 0.0, jnp.where(code < 0.0, -size, size))
 
 
 def mod4(v):
@@ -31,8 +47,8 @@
     s0, s1, s2, fp0, fp1, fp2, own0, own1, own2, hb0, hb1, hb2, rb0, rb1, rb2,
     r2a0, r2a1, r2a2, r2b0, r2b1, r2b2, r2s0, r2s1, r2s2,
     r3b0, r3b1, r3b2,
-    wfull, wlow, w1b0, w1b1, w1b2, wp0, wp1, wp2, w2b0, w2b1, w2b2, w3b0, w3b1, w3b2, wout,
-    load_sem, ag_s, ag_r, rs_s, rs_r, wt_s, wt_r, d2d_s, d2d_r, out_sem,
+    wfull, wlow, w1b0, w1b1, w1b2, wp0, wp1, wp2, wc0, wc1, wc2, w2b0, w2b1, w2b2, w3b0, w3b1, w3b2, wout, wsib,
+    load_sem, ag_s, ag_r, rs_s, rs_r, wt_s, wt_r, d2d_s, d2d_r, out_s, out_r,
 ):
     g, i = lax.axis_index("group"), lax.axis_index("inner")
     x = (i // 8) * 2 + g // 4
@@ -94,24 +110,34 @@
     pl.semaphore_wait(barrier, len(partners))
 
     def own_block():
-        for off in OFFS:
-            for p in range(3):
-                a, b, c = PARTS[p]
-                send(table.at[:, cols(p)], row_of(tab, p, 0, 0, BACK[off]), ag_s.at[p], ag_r.at[p, 15], peer(a, off))
+        for p in range(3):
+            a, b, c = PARTS[p]
+            block = table.at[:, cols(p)]
+            for off in OFFS:
+                send(block, row_of(tab, p, 0, 0, BACK[off]), ag_s.at[p], ag_r.at[p, 12], peer(a, off))
+        for p in range(3):
+            a, b, c = PARTS[p]
+            block = table.at[:, cols(p)]
+            for k, off in enumerate(OFFS):
+                send(block, row_of(tab, p, BACK[off], 0, 0), ag_s.at[p], ag_r.at[p, k], peer(b, off))
+            for d, off in enumerate((1, -1)):
+                send(block, row_of(tab, p, 0, BACK[off], 0), ag_s.at[p], ag_r.at[p, 3 + d], peer(c, off))
 
     def send_row_c(p, j):
+        part = slice(None) if j else slice(1, 4)
         for d, off in enumerate((1, -1)):
-            to = row_of(tab, p, j, BACK[off])
-            send(row_of(tab, p, j, 0), to, ag_s.at[p], ag_r.at[p, 3 + 2 * j + d], peer(PARTS[p][2], off))
+            to = row_of(tab, p, j, BACK[off], part)
+            send(row_of(tab, p, j, 0, part), to, ag_s.at[p], ag_r.at[p, 3 + 2 * j + d], peer(PARTS[p][2], off))
 
     def own_row():
         loads[0].wait()
-        for p in range(3):
-            received(row_of(tab, p, 0, 0, slice(1, 4)), ag_r.at[p, 15])
+        rest = slice(1, 4)
+        for p in range(3):
+            received(row_of(tab, p, 0, 0, rest), ag_r.at[p, 12])
         for p in range(3):
             for k, off in enumerate(OFFS):
-                to = row_of(tab, p, BACK[off], 0)
-                send(row_of(tab, p, 0, 0), to, ag_s.at[p], ag_r.at[p, k], peer(PARTS[p][1], off))
+                to = row_of(tab, p, BACK[off], 0, rest)
+                send(row_of(tab, p, 0, 0, rest), to, ag_s.at[p], ag_r.at[p, k], peer(PARTS[p][1], off))
             send_row_c(p, 0)
 
     def rows_of_b():
@@ -126,12 +152,11 @@
                 row = row_of(tab, p, j, BACK[off])
                 received(row, ag_r.at[p, 3 + 2 * j + d])
                 if (j in (0, 1)) == (d == 0):
-                    send(row, row_of(tab, p, j, 3), ag_s.at[p], ag_r.at[p, 11 + j], peer(PARTS[p][2], off))
+                    send(row, row_of(tab, p, j, 3), ag_s.at[p], ag_r.at[p, 11], peer(PARTS[p][2], off))
 
     def far_rows():
-        for j in range(4):
-            for p in range(3):
-                received(row_of(tab, p, j, 3), ag_r.at[p, 11 + j])
+        for p in range(3):
+            received(row_of(tab, p, slice(None), 3), ag_r.at[p, 11])
 
     def hidden_of(rows):
         hidden = lax.dot_general(w_t[...], vis[rows, :], NT, preferred_element_type=F32)
@@ -171,9 +196,8 @@
             value = (prob - jnp.where(gap == 0.0, 1.0, 0.0)) * scale
             res[zs, ys, xs, :, seen] = value.astype(BF16).reshape(*shape, 32, 512)
 
-    def turn(n, _):
-        tab_t[:, pl.ds(pl.multiple_of(n * 512, 512), 512)] = tab[n].reshape(512, 1024).T
-        return 0
+    def turn(n):
+        tab_t[:, pl.ds(n * 512, 512)] = tab[n].reshape(512, 1024).T
 
     near, far, all_of = slice(0, 3), slice(3, 4), slice(0, 4)
 
@@ -207,24 +231,24 @@
     for n in range(3):
         residual_of(slice(n, n + 1), near, near)
     far_rows()
+    turn(3)
     residual_of(far, all_of, all_of)
+    turn(0)
+    turn(1)
     residual_of(near, far, all_of)
+    turn(2)
     residual_of(near, near, far)
-    lax.fori_loop(0, 4, turn, 0)
 
     flat = res.reshape(2048, 1024)
 
-    def coded_grad(at):
-        rows = tab_t[pl.ds(pl.multiple_of(at, 128), 128), :]
-        return lax.dot_general(rows, flat[...], NN, preferred_element_type=F32)
-
-    def away(n, _):
-        part = pl.ds(pl.multiple_of(n * 128, 128), 128)
-        cg_out[part, :] = coded_grad((1 - core) * 512 + n * 128).astype(BF16)
-        send(cg_out.at[part], cg_in.at[part], d2d_s.at[3], d2d_r.at[3], sibling)
-        return 0
-
-    lax.fori_loop(0, 4, away, 0)
+    def coded_grad(rows, seen):
+        return lax.dot_general(tab_t[rows, :], flat[:, seen], NN, preferred_element_type=F32)
+
+    def away():
+        for n in range(2):
+            seen = pl.ds(n * 512, 512)
+            cg_out[:, seen] = coded_grad(theirs, seen).astype(BF16)
+            send(cg_out.at[:, seen], cg_in.at[:, seen], d2d_s.at[3], d2d_r.at[3], sibling)
 
     s, fp, own = (s0, s1, s2), (fp0, fp1, fp2), (own0, own1, own2)
     hb, rb = (hb0, hb1, hb2), (rb0, rb1, rb2)
@@ -235,25 +259,24 @@
         value = lax.dot_general(rows, coded[cols(p), :], NT, preferred_element_type=F32)
         return value.reshape(4, 4, 32, COLS[p][1])
 
-    for p in range(3):
-        s[p][2] = term(p, 3).astype(BF16)
-        for j in range(4):
-            src = plane_row(s[p].at[2], p, j)
-            send(src, hb[p].at[j], rs_s.at[p, 0], rs_r.at[p, j], peer(PARTS[p][2], 1 if j < 2 else -1))
-
-    def home(n, _):
-        cg_own[pl.ds(pl.multiple_of(n * 128, 128), 128), :] = coded_grad(core * 512 + n * 128)
-        return 0
-
-    lax.fori_loop(0, 4, home, 0)
-    received(cg_in, d2d_r.at[3])
-    hgrad[...] = ((cg_own[...] + cg_in[...].astype(F32)) * (1.0 - squash[...] * squash[...])).astype(BF16)
-
-    for half in range(2):
-        value = lax.dot_general(vis_t[pl.ds(half * 512, 512), :], hgrad[...], NT, preferred_element_type=F32)
-        wfull[:, pl.ds(half * 512, 512)] = value
-        wlow[:, pl.ds(half * 512, 512)] = value.astype(BF16)
-    w1b, wp, w2b, w3b = (w1b0, w1b1, w1b2), (wp0, wp1, wp2), (w2b0, w2b1, w2b2), (w3b0, w3b1, w3b2)
+    def far_terms():
+        for p in range(3):
+            s[p][2] = term(p, 3).astype(BF16)
+            for j in range(4):
+                src = plane_row(s[p].at[2], p, j)
+                send(src, hb[p].at[j], rs_s.at[p, 0], rs_r.at[p, j], peer(PARTS[p][2], 1 if j < 2 else -1))
+
+    def weight_terms():
+        cg_own[...] = coded_grad(mine, slice(None))
+        received(cg_in, d2d_r.at[3])
+        hgrad[...] = ((cg_own[...] + cg_in[...].astype(F32)) * (1.0 - squash[...] * squash[...])).astype(BF16)
+        for half in range(2):
+            value = lax.dot_general(vis_t[pl.ds(half * 512, 512), :], hgrad[...], NT, preferred_element_type=F32)
+            wfull[:, pl.ds(half * 512, 512)] = value
+            wlow[:, pl.ds(half * 512, 512)] = value.astype(BF16)
+
+    w1b, wp, wc = (w1b0, w1b1, w1b2), (wp0, wp1, wp2), (wc0, wc1, wc2)
+    w2b, w3b = (w2b0, w2b1, w2b2), (w3b0, w3b1, w3b2)
 
     def span(at, size):
         return pl.ds(pl.multiple_of(at * size, size), size)
@@ -261,7 +284,8 @@
     def w_row(c_at, b_at):
         return span(c_at * 4 + b_at, 32)
 
-    for j in (1, 2, 3, 0):
+    def w_send_rows():
+      for j in (1, 2, 3, 0):
         for k, off in enumerate(OFFS):
             for p in range(3):
                 a, b, c = PARTS[p]
@@ -273,18 +297,21 @@
             for p in range(3):
                 a, b, c = PARTS[p]
                 received(w1b[p].at[j], wt_r.at[p, j])
-                wp[p][j] = (
+                whole = (
                     wfull[w_row(pos[c], places[b, REL[j]]), cols(p)]
                     + w1b[p][j, 0].astype(F32) + w1b[p][j, 1].astype(F32) + w1b[p][j, 2].astype(F32)
                 )
                 if j:
-                    send(wp[p].at[j], w2b[p].at[j - 1], wt_s.at[p, 1], wt_r.at[p, 4], peer(b, REL[j]))
+                    wc[p][j - 1] = encode(whole)
+                    send(wc[p].at[j - 1], w2b[p].at[j - 1], wt_s.at[p, 1], wt_r.at[p, 4], peer(b, REL[j]))
+                else:
+                    wp[p][...] = whole
 
     def w_sum_b():
         for p in range(3):
             a, b, c = PARTS[p]
             received(w2b[p], wt_r.at[p, 4])
-            w3b[p][pos[a]] = wp[p][0] + w2b[p][0] + w2b[p][1] + w2b[p][2]
+            w3b[p][pos[a]] = encode(wp[p][...] + decode(w2b[p][0]) + decode(w2b[p][1]) + decode(w2b[p][2]))
             own_slot = w3b[p].at[pos[a]]
             for off in OFFS:
                 send(own_slot, own_slot, wt_s.at[p, 1], wt_r.at[p, 5], peer(a, off))
@@ -300,7 +327,7 @@
             a, b, c = PARTS[p]
             received(w3b[p].at[pl.ds(0, 3)], wt_r.at[p, 5])
             at = w_row(0, pos[b])
-            wout[at, cols(p)] = w3b[p][0] + w3b[p][1] + w3b[p][2] + w3b[p][3]
+            wout[at, cols(p)] = encode(decode(w3b[p][0]) + decode(w3b[p][1]) + decode(w3b[p][2]) + decode(w3b[p][3]))
             row = wout.at[at, cols(p)]
             for k, off in enumerate(OFFS):
                 send(row, row, wt_s.at[p, 2], wt_r.at[p, 6 + k], peer(b, off))
@@ -309,15 +336,24 @@
     pieces = (((0, 0, 384),), ((384, 0, 128), (512, 1, 256)), ((768, 1, 256),))
 
     def deliver(p, at):
+        src = wout.at[pl.ds(at * 128, 128), cols(p)]
+        send(src, wsib.at[pl.ds(at * 128, 128), cols(p)], out_s.at[0], out_r.at[p, at], sibling)
+
+    def put(buf, column, p, at):
         c_at = places[PARTS[p][2], REL[at]]
         for lo, half, size in pieces[p]:
-            src = wout.at[pl.ds(at * 128, 128), pl.ds(lo, size)]
-            dst = wgrad.at[
-                pl.ds(pl.multiple_of(half * 512 + c_at * 128, 128), 128),
-                pl.ds(pl.multiple_of(core * 512 + lo - half * 512, 128), size),
-            ]
-            pltpu.make_async_copy(src, dst, out_sem.at[0]).start()
-            send(src, dst, out_sem.at[1], out_sem.at[2], sibling)
+            rows = pl.ds(pl.multiple_of(half * 512 + c_at * 128, 128), 128)
+            lanes = pl.ds(pl.multiple_of(column * 512 + lo - half * 512, 128), size)
+            wgrad[rows, lanes] = decode(buf[pl.ds(at * 128, 128), pl.ds(lo, size)])
+
+    def put_own(at):
+        for p in range(3):
+            put(wout, core, p, at)
+
+    def put_sibling(at):
+        for p in range(3):
+            received(wsib.at[pl.ds(at * 128, 128), cols(p)], out_r.at[p, at])
+            put(wsib, 1 - core, p, at)
 
     def w_take_b():
         for k, off in enumerate(OFFS):
@@ -337,20 +373,19 @@
                     received(row, wt_r.at[p, 9 + 2 * j + d])
                     if (j in (0, 1)) == (d == 0):
                         to = wout.at[w_row(3, places[b, REL[j]]), cols(p)]
-                        send(row, to, wt_s.at[p, 2], wt_r.at[p, 17 + j], peer(c, off))
+                        send(row, to, wt_s.at[p, 2], wt_r.at[p, 17], peer(c, off))
         for p in range(3):
             deliver(p, 1)
             deliver(p, 2)
 
     def w_take_far():
         for p in range(3):
-            for j in range(4):
-                received(wout.at[w_row(3, places[PARTS[p][1], REL[j]]), cols(p)], wt_r.at[p, 17 + j])
+            received(wout.at[pl.ds(384, 128), cols(p)], wt_r.at[p, 17])
             deliver(p, 3)
 
     def send_term_row(p, k, j):
         src = plane_row(s[p].at[k], p, j)
-        send(src, rb[p].at[k, j], rs_s.at[p, 0], rs_r.at[p, 4 + 4 * k + j], peer(PARTS[p][2], OFFS[k]))
+        send(src, rb[p].at[k, j], rs_s.at[p, 0], rs_r.at[p, 4], peer(PARTS[p][2], OFFS[k]))
 
     def near_terms(k):
         for p in range(3):
@@ -374,51 +409,62 @@
 
     def sum_c(p):
         a, b, c = PARTS[p]
-        for j in (2, 0, 1, 3):
-            for k in range(2):
-                received(rb[p].at[k, j], rs_r.at[p, 4 + 4 * k + j])
+        received(rb[p], rs_r.at[p, 4])
+        for j in range(4):
             mine_row = plane_row(own[p], p, j)
             mine_row[...] = mine_row[...] + rb[p][0, j].astype(F32) + rb[p][1, j].astype(F32)
         r2a[p][...] = own[p][...].astype(BF16)
         for k, off in enumerate(OFFS):
             src = plane_row(r2a[p], p, REL.index(off))
-            send(src, r2b[p].at[k], rs_s.at[p, 0], rs_r.at[p, 12], peer(b, off))
+            send(src, r2b[p].at[k], rs_s.at[p, 0], rs_r.at[p, 5], peer(b, off))
 
     def sum_b():
         for p in range(3):
             a, b, c = PARTS[p]
-            received(r2b[p], rs_r.at[p, 12])
+            received(r2b[p], rs_r.at[p, 5])
             r2s[p][...] = (
                 plane_row(own[p], p, 0)[...]
                 + r2b[p][0].astype(F32) + r2b[p][1].astype(F32) + r2b[p][2].astype(F32)
             )
             for k, off in enumerate(OFFS):
-                send(r2s[p].at[REL.index(off)], r3b[p].at[k], rs_s.at[p, 1], rs_r.at[p, 13], peer(a, off))
+                send(r2s[p].at[REL.index(off)], r3b[p].at[k], rs_s.at[p, 1], rs_r.at[p, 6], peer(a, off))
 
     def sum_a():
         for p in range(3):
             a, b, c = PARTS[p]
-            received(r3b[p], rs_r.at[p, 13])
+            received(r3b[p], rs_r.at[p, 6])
             dgrad[:, cols(p)] = r2s[p][0] + r3b[p][0] + r3b[p][1] + r3b[p][2]
 
+    far_terms()
     near_terms(0)
     near_terms(1)
-    w_sum_c()
-    own_terms()
+    away()
     pass_on(0)
     pass_on(2)
-    w_sum_b()
     pass_on(1)
     pass_on(3)
+    weight_terms()
+    w_send_rows()
+    own_terms()
+    w_sum_c()
+    sum_c(0)
+    w_sum_b()
+    sum_c(1)
     w_sum_a()
-    sum_c(0)
+    sum_c(2)
     w_take_b()
-    sum_c(1)
-    sum_c(2)
+    sum_b()
     w_take_c()
-    sum_b()
+    put_own(0)
+    put_own(1)
+    put_own(2)
+    put_sibling(0)
+    sum_a()
+    put_sibling(1)
+    put_sibling(2)
     w_take_far()
-    sum_a()
+    put_own(3)
+    put_sibling(3)
 
     flat_tab = tab.reshape(64, 32, 1024)
     for p in range(3):
@@ -430,8 +476,15 @@
         received(wout.at[pl.ds(0, 480), cols(p)], wt_s.at[p, 2])
     for n, ref in enumerate((vis.at[mine], lab.at[mine], coded.at[mine], cg_out)):
         received(ref, d2d_s.at[n])
-    for n in range(3):
-        received(wout, out_sem.at[n])
+    received(wout, out_s.at[0])
+
+
+def write_out(dgrad, wgrad, dgrad_out, wgrad_out, sem):
+    copies = [pltpu.make_async_copy(dgrad, dgrad_out, sem.at[0]), pltpu.make_async_copy(wgrad, wgrad_out, sem.at[1])]
+    for copy in copies:
+        copy.start()
+    for copy in copies:
+        copy.wait()
 
 
 def per_part(make):
@@ -457,18 +510,19 @@
         *per_part(lambda n: vmem((3, 32, n), F32)),
         vmem((512, 1024), F32), vmem((512, 1024), BF16),
         *per_part(lambda n: vmem((4, 3, 32, n), BF16)),
-        *per_part(lambda n: vmem((4, 32, n), F32)),
-        *per_part(lambda n: vmem((3, 32, n), F32)),
-        *per_part(lambda n: vmem((4, 32, n), F32)),
-        vmem((512, 1024), F32),
+        *per_part(lambda n: vmem((32, n), F32)),
+        *per_part(lambda n: vmem((3, 32, n), jnp.int16)),
+        *per_part(lambda n: vmem((3, 32, n), jnp.int16)),
+        *per_part(lambda n: vmem((4, 32, n), jnp.int16)),
+        vmem((512, 1024), jnp.int16), vmem((512, 1024), jnp.int16),
         pltpu.SemaphoreType.DMA((5,)),
-        pltpu.SemaphoreType.DMA((3,)), pltpu.SemaphoreType.DMA((3, 16)),
-        pltpu.SemaphoreType.DMA((3, 2)), pltpu.SemaphoreType.DMA((3, 14)),
-        pltpu.SemaphoreType.DMA((3, 3)), pltpu.SemaphoreType.DMA((3, 21)),
-        pltpu.SemaphoreType.DMA((4,)), pltpu.SemaphoreType.DMA((4,)), pltpu.SemaphoreType.DMA((3,)),
+        pltpu.SemaphoreType.DMA((3,)), pltpu.SemaphoreType.DMA((3, 13)),
+        pltpu.SemaphoreType.DMA((3, 2)), pltpu.SemaphoreType.DMA((3, 7)),
+        pltpu.SemaphoreType.DMA((3, 3)), pltpu.SemaphoreType.DMA((3, 18)),
+        pltpu.SemaphoreType.DMA((4,)), pltpu.SemaphoreType.DMA((4,)), pltpu.SemaphoreType.DMA((1,)), pltpu.SemaphoreType.DMA((3, 4)),
     ]
     anywhere = pl.BlockSpec(memory_space=pl.ANY)
-    return pl.pallas_call(
+    drug_grad, weight_grad = pl.pallas_call(
         kernel,
         name="step",
         out_shape=(pltpu.VMEM((32, 1024), F32), pltpu.VMEM((1024, 1024), F32)),
@@ -479,6 +533,15 @@
             collective_id=0, has_side_effects=True, vmem_limit_bytes=54 * 2**20
         ),
     )(visits, enc_weight, drug_table, labels.T, drug_order.reshape(32, 128))
+    return pl.pallas_call(
+        write_out,
+        name="write_out",
+        out_shape=(jax.ShapeDtypeStruct((32, 1024), F32), jax.ShapeDtypeStruct((1024, 1024), F32)),
+        in_specs=[pl.BlockSpec(memory_space=pltpu.VMEM)] * 2,
+        out_specs=[anywhere] * 2,
+        scratch_shapes=[pltpu.SemaphoreType.DMA((2,))],
+        compiler_params=pltpu.CompilerParams(vmem_limit_bytes=2**20),
+    )(drug_grad, weight_grad)
 
 
 def solution(mesh):

time: 87.7 us -> 80.1 us (0.913)
  Pallas kernels: 83.9 us -> 79.2 us
  local copies, waits for them, and re-layouts: 2.67 us -> 0 us
    pallas_call x1, Pallas kernels: 83.9 us -> 77.1 us  [local(): pl.pallas_call(kernel, name='step', out_shape=(pltpu.VMEM((32, 1024), F32...]
    unnamed x2 -> x0, local copies, waits for them, and re-layouts: 2.67 us -> none
    pallas_call x0 -> x1, Pallas kernels: none -> 2.08 us  [local(): pl.pallas_call(write_out, name='write_out', out_shape=(jax.ShapeDtypeStru...]
where the time goes in v4:
time: 80.1 us; the launch traced here: 80 us
  Pallas kernels  79.2 us (99%)
    pallas_call x1, Pallas kernels, local(): pl.pallas_call(kernel, name='step', out_shape=(pltpu.VMEM((32, 1024), F32...  77.1 us
    pallas_call x1, Pallas kernels, local(): pl.pallas_call(write_out, name='write_out', out_shape=(jax.ShapeDtypeStru...  2.08 us

profile of v4, /device:TPU:1, one launch (start us, length us, event | category | flops | bytes accessed | tf_op | source)
XLA Modules:
  0.0 80.0 jit_solution(3440331287889004645)
XLA Ops:
  0.6 77.1 %step.1 = (f32[32,1024]{1,0:T(8,128)S(1)}, f32[1024,1024]{1,0:T(8,128)S(1)}) custom-call(bf16[512,1024]{1,0:T(8,128)(2,1)} %visits.1, bf16[1024,1024]{1,0:T(8,128)(2,1)} %weight.1, bf16[32,1024]{1,0:T(8,128)(2,1)} %table.1, s32[32,512]{1,0:T(8,128)} %bitcast.2, s32[32,128]{1,0:T(8,128)} %bitcast.3), custom_call_target="tpu_custom_call" | custom-call | tf_op jit(solution)/shard_map/step/pallas_call | solution.py:525
  77.7 2.1 %write_out.1 = (f32[32,1024]{1,0:T(8,128)}, f32[1024,1024]{1,0:T(8,128)}) custom-call(f32[32,1024]{1,0:T(8,128)S(1)} %get-tuple-element.4.dgrad, f32[1024,1024]{1,0:T(8,128)S(1)} %get-tuple-element.5.wgrad), custom_call_target="tpu_custom_call" | custom-call | tf_op jit(solution)/shard_map/write_out/pallas_call | solution.py:536

commit v5 on v4

--- a/solution.py
+++ b/solution.py
@@ -17,6 +17,7 @@
 COLS = ((0, 384), (384, 384), (768, 256))
 OFFS = (1, -1, 2)
 REL = (0, 1, -1, 2)
+PAIRS = (slice(0, 2), slice(2, 4))
 BACK = {1: 2, -1: 1, 2: 3}
 
 
@@ -140,8 +141,9 @@
                 send(row_of(tab, p, 0, 0, rest), to, ag_s.at[p], ag_r.at[p, k], peer(PARTS[p][1], off))
             send_row_c(p, 0)
 
-    def rows_of_b():
-        for k, off in enumerate(OFFS):
+    def rows_of_b(steps):
+        for k in steps:
+            off = OFFS[k]
             for p in range(3):
                 received(row_of(tab, p, BACK[off], 0), ag_r.at[p, k])
                 send_row_c(p, BACK[off])
@@ -151,8 +153,9 @@
             for d, off in enumerate((1, -1)):
                 row = row_of(tab, p, j, BACK[off])
                 received(row, ag_r.at[p, 3 + 2 * j + d])
-                if (j in (0, 1)) == (d == 0):
-                    send(row, row_of(tab, p, j, 3), ag_s.at[p], ag_r.at[p, 11], peer(PARTS[p][2], off))
+                part = slice(2 * d, 2 * d + 2)
+                half = row_of(tab, p, j, BACK[off], part)
+                send(half, row_of(tab, p, j, 3, part), ag_s.at[p], ag_r.at[p, 11], peer(PARTS[p][2], off))
 
     def far_rows():
         for p in range(3):
@@ -213,17 +216,18 @@
     w_t[...] = w_half[...].T
     loads[2].wait()
     hidden_of(mine)
-    rows_of_b()
+    rows_of_b((0, 1))
+    rows_of_c(0)
     received(vis.at[theirs], d2d_r.at[0])
     hidden_of(theirs)
     send(coded.at[mine], coded.at[mine], d2d_s.at[2], d2d_r.at[2], sibling)
-    rows_of_c(0)
+    rows_of_b((2,))
     loads[4].wait()
     order_t[...] = own_order[...].astype(F32).T
     lax.fori_loop(0, 64, select, 0)
+    rows_of_c(1)
+    vis_t[...] = vis[...].T
     rows_of_c(2)
-    vis_t[...] = vis[...].T
-    rows_of_c(1)
     rows_of_c(3)
     received(coded.at[theirs], d2d_r.at[2])
     received(lab.at[theirs], d2d_r.at[1])
@@ -262,9 +266,9 @@
     def far_terms():
         for p in range(3):
             s[p][2] = term(p, 3).astype(BF16)
-            for j in range(4):
-                src = plane_row(s[p].at[2], p, j)
-                send(src, hb[p].at[j], rs_s.at[p, 0], rs_r.at[p, j], peer(PARTS[p][2], 1 if j < 2 else -1))
+            for k, pair in enumerate(PAIRS):
+                src = plane_row(s[p].at[2], p, pair)
+                send(src, plane_row(hb[p], p, pair), rs_s.at[p, 0], rs_r.at[p, k], peer(PARTS[p][2], OFFS[k]))
 
     def weight_terms():
         cg_own[...] = coded_grad(mine, slice(None))
@@ -365,15 +369,15 @@
             deliver(p, 0)
 
     def w_take_c():
-        for j in (0, 2, 1, 3):
+        for j in range(4):
             for p in range(3):
                 a, b, c = PARTS[p]
                 for d, off in enumerate((1, -1)):
                     row = wout.at[w_row(BACK[off], places[b, REL[j]]), cols(p)]
                     received(row, wt_r.at[p, 9 + 2 * j + d])
-                    if (j in (0, 1)) == (d == 0):
-                        to = wout.at[w_row(3, places[b, REL[j]]), cols(p)]
-                        send(row, to, wt_s.at[p, 2], wt_r.at[p, 17], peer(c, off))
+                    here = pl.ds(pl.multiple_of((BACK[off] * 4 + places[b, REL[j]]) * 32 + 16 * d, 16), 16)
+                    there = pl.ds(pl.multiple_of((12 + places[b, REL[j]]) * 32 + 16 * d, 16), 16)
+                    send(wout.at[here, cols(p)], wout.at[there, cols(p)], wt_s.at[p, 2], wt_r.at[p, 17], peer(c, off))
         for p in range(3):
             deliver(p, 1)
             deliver(p, 2)
@@ -383,36 +387,33 @@
             received(wout.at[pl.ds(384, 128), cols(p)], wt_r.at[p, 17])
             deliver(p, 3)
 
-    def send_term_row(p, k, j):
-        src = plane_row(s[p].at[k], p, j)
-        send(src, rb[p].at[k, j], rs_s.at[p, 0], rs_r.at[p, 4], peer(PARTS[p][2], OFFS[k]))
+    def send_term_rows(p, k, pair):
+        src = plane_row(s[p].at[k], p, pair)
+        send(src, plane_row(rb[p].at[k], p, pair), rs_s.at[p, 0], rs_r.at[p, 4], peer(PARTS[p][2], OFFS[k]))
 
     def near_terms(k):
         for p in range(3):
             value = term(p, 1 + k)
             fp[p][k] = value
             s[p][k] = value.astype(BF16)
-            for j in (2, 3) if k == 0 else (0, 1):
-                send_term_row(p, k, j)
-
-    def pass_on(j):
-        k = 0 if j < 2 else 1
-        for p in range(3):
-            received(hb[p].at[j], rs_r.at[p, j])
-            whole = plane_row(fp[p].at[k], p, j)[...] + hb[p][j].astype(F32)
-            plane_row(s[p].at[k], p, j)[...] = whole.astype(BF16)
-            send_term_row(p, k, j)
+            send_term_rows(p, k, PAIRS[1 - k])
+
+    def pass_on(k):
+        pair = PAIRS[k]
+        for p in range(3):
+            received(plane_row(hb[p], p, pair), rs_r.at[p, k])
+            whole = plane_row(fp[p].at[k], p, pair)[...] + plane_row(hb[p], p, pair)[...].astype(F32)
+            plane_row(s[p].at[k], p, pair)[...] = whole.astype(BF16)
+            send_term_rows(p, k, pair)
 
     def own_terms():
         for p in range(3):
             own[p][...] = term(p, 0)
 
     def sum_c(p):
-        a, b, c = PARTS[p]
+        b = PARTS[p][1]
         received(rb[p], rs_r.at[p, 4])
-        for j in range(4):
-            mine_row = plane_row(own[p], p, j)
-            mine_row[...] = mine_row[...] + rb[p][0, j].astype(F32) + rb[p][1, j].astype(F32)
+        own[p][...] = own[p][...] + rb[p][0].astype(F32) + rb[p][1].astype(F32)
         r2a[p][...] = own[p][...].astype(BF16)
         for k, off in enumerate(OFFS):
             src = plane_row(r2a[p], p, REL.index(off))
@@ -440,18 +441,16 @@
     near_terms(1)
     away()
     pass_on(0)
-    pass_on(2)
     pass_on(1)
-    pass_on(3)
     weight_terms()
     w_send_rows()
     own_terms()
     w_sum_c()
+    w_sum_b()
     sum_c(0)
-    w_sum_b()
     sum_c(1)
+    sum_c(2)
     w_sum_a()
-    sum_c(2)
     w_take_b()
     sum_b()
     w_take_c()

time: 80.1 us -> 78.9 us (0.985)
  Pallas kernels: 79.2 us -> 78 us
    pallas_call x1, Pallas kernels: 77.1 us -> 75.9 us  [local(): pl.pallas_call(kernel, name='step', out_shape=(pltpu.VMEM((32, 1024), F32...]
where the time goes in v5:
time: 78.9 us; the launch traced here: 78.8 us
  Pallas kernels  78 us (99%)
  between operations  0.8 us (1%)
    pallas_call x1, Pallas kernels, local(): pl.pallas_call(kernel, name='step', out_shape=(pltpu.VMEM((32, 1024), F32...  75.9 us
    pallas_call x1, Pallas kernels, local(): pl.pallas_call(write_out, name='write_out', out_shape=(jax.ShapeDtypeStru...  2.08 us

profile of v5, /device:TPU:1, one launch (start us, length us, event | category | flops | bytes accessed | tf_op | source)
XLA Modules:
  0.0 78.8 jit_solution(4952392050221864325)
XLA Ops:
  0.6 75.9 %step.1 = (f32[32,1024]{1,0:T(8,128)S(1)}, f32[1024,1024]{1,0:T(8,128)S(1)}) custom-call(bf16[512,1024]{1,0:T(8,128)(2,1)} %visits.1, bf16[1024,1024]{1,0:T(8,128)(2,1)} %weight.1, bf16[32,1024]{1,0:T(8,128)(2,1)} %table.1, s32[32,512]{1,0:T(8,128)} %bitcast.2, s32[32,128]{1,0:T(8,128)} %bitcast.3), custom_call_target="tpu_custom_call" | custom-call | tf_op jit(solution)/shard_map/step/pallas_call | solution.py:524
  76.5 2.1 %write_out.1 = (f32[32,1024]{1,0:T(8,128)}, f32[1024,1024]{1,0:T(8,128)}) custom-call(f32[32,1024]{1,0:T(8,128)S(1)} %get-tuple-element.4.dgrad, f32[1024,1024]{1,0:T(8,128)S(1)} %get-tuple-element.5.wgrad), custom_call_target="tpu_custom_call" | custom-call | tf_op jit(solution)/shard_map/write_out/pallas_call | solution.py:535

commit v6 on v5

--- a/solution.py
+++ b/solution.py
@@ -278,6 +278,7 @@
             value = lax.dot_general(vis_t[pl.ds(half * 512, 512), :], hgrad[...], NT, preferred_element_type=F32)
             wfull[:, pl.ds(half * 512, 512)] = value
             wlow[:, pl.ds(half * 512, 512)] = value.astype(BF16)
+            w_send_rows((1, 2) if half else (0,))
 
     w1b, wp, wc = (w1b0, w1b1, w1b2), (wp0, wp1, wp2), (wc0, wc1, wc2)
     w2b, w3b = (w2b0, w2b1, w2b2), (w3b0, w3b1, w3b2)
@@ -288,13 +289,13 @@
     def w_row(c_at, b_at):
         return span(c_at * 4 + b_at, 32)
 
-    def w_send_rows():
-      for j in (1, 2, 3, 0):
-        for k, off in enumerate(OFFS):
-            for p in range(3):
-                a, b, c = PARTS[p]
-                src = wlow.at[w_row(places[c, off], places[b, REL[j]]), cols(p)]
-                send(src, w1b[p].at[j, k], wt_s.at[p, 0], wt_r.at[p, j], peer(c, off))
+    def w_send_rows(parts):
+        for j in (1, 2, 3, 0):
+            for k, off in enumerate(OFFS):
+                for p in parts:
+                    a, b, c = PARTS[p]
+                    src = wlow.at[w_row(places[c, off], places[b, REL[j]]), cols(p)]
+                    send(src, w1b[p].at[j, k], wt_s.at[p, 0], wt_r.at[p, j], peer(c, off))
 
     def w_sum_c():
         for j in (1, 2, 3, 0):
@@ -443,7 +444,6 @@
     pass_on(0)
     pass_on(1)
     weight_terms()
-    w_send_rows()
     own_terms()
     w_sum_c()
     w_sum_b()

time: 78.9 us -> 79 us (level)
  no operation moved by 1% of the time
where the time goes in v6:
time: 79 us; the launch traced here: 78.9 us
  Pallas kernels  78.1 us (99%)
  between operations  0.8 us (1%)
    pallas_call x1, Pallas kernels, local(): pl.pallas_call(kernel, name='step', out_shape=(pltpu.VMEM((32, 1024), F32...  76 us
    pallas_call x1, Pallas kernels, local(): pl.pallas_call(write_out, name='write_out', out_shape=(jax.ShapeDtypeStru...  2.08 us

profile of v6, /device:TPU:1, one launch (start us, length us, event | category | flops | bytes accessed | tf_op | source)
XLA Modules:
  0.0 78.9 jit_solution(16960092201208392660)
XLA Ops:
  0.6 76.0 %step.1 = (f32[32,1024]{1,0:T(8,128)S(1)}, f32[1024,1024]{1,0:T(8,128)S(1)}) custom-call(bf16[512,1024]{1,0:T(8,128)(2,1)} %visits.1, bf16[1024,1024]{1,0:T(8,128)(2,1)} %weight.1, bf16[32,1024]{1,0:T(8,128)(2,1)} %table.1, s32[32,512]{1,0:T(8,128)} %bitcast.2, s32[32,128]{1,0:T(8,128)} %bitcast.3), custom_call_target="tpu_custom_call" | custom-call | tf_op jit(solution)/shard_map/step/pallas_call | solution.py:524
  76.7 2.1 %write_out.1 = (f32[32,1024]{1,0:T(8,128)}, f32[1024,1024]{1,0:T(8,128)}) custom-call(f32[32,1024]{1,0:T(8,128)S(1)} %get-tuple-element.4.dgrad, f32[1024,1024]{1,0:T(8,128)S(1)} %get-tuple-element.5.wgrad), custom_call_target="tpu_custom_call" | custom-call | tf_op jit(solution)/shard_map/write_out/pallas_call | solution.py:535
